TPU v7x, 128 devices: a whole 4x4x4 slice. The times are simulated.
128 devices in a mesh: dp: 32 (over x, z, y_hi), space: 4 (over y_lo, core).
Axes of the slice: x: 4, y: 4 (y_hi: 2, y_lo: 2; y = y_hi * 2 + y_lo), z: 4, core: 2. Of those that a mesh axis runs over, the one named last changes fastest.
Arguments:
- features: bfloat16 [32, 48, 56, 1024], P('dp', 'space'), may hold values from -6 to 6
- labels: int32 [32, 48, 56], P('dp', 'space'), may hold values from 0 to 2
- w_one: bfloat16 [1024, 256], replicated, may hold values from -0.1875 to 0.1875
- w_atrous: bfloat16 [2, 3, 3, 1024, 256], replicated, may hold values from -0.0625 to 0.0625
- w_proj: bfloat16 [768, 256], replicated, may hold values from -0.21875 to 0.21875
- w_class: bfloat16 [256, 3], replicated, may hold values from -1.5 to 1.5
Outputs:
- grad_atrous: float32 [2, 3, 3, 1024, 256], P(None, None, None, ('dp', 'space'))
- grad_one: float32 [1024, 256], replicated
- grad_proj: float32 [768, 256], replicated
- grad_class: float32 [256, 3], replicated
- mean_loss: float32 [], replicated
All inputs are finite; a program needn't handle non-finite values.
Results may differ from a plain program's by a relative error of at most 0.0043.
Values may be sent and summed in bfloat16 or wider, within the bound.
A program may use at most 192 MiB of HBM per device.

v0:
```python
import math

import jax
import jax.numpy as jnp
from jax import lax
from jax.sharding import PartitionSpec as P

RATE_A = 12
RATE_B = 18


def from_behind(value, axis, steps):
    count = lax.axis_size(axis)
    first, last = (max(0, -steps), min(count, count - steps))
    return lax.ppermute(value, axis, [(source, source + steps) for source in range(first, last)])


def silu_slope(pre):
    gate = jax.nn.sigmoid(pre)
    return gate * (1.0 + pre * (1.0 - gate))


def atrous_sum(padded, weights, rate, height, width, margin):
    summed = jnp.zeros((height * width, weights.shape[-1]), jnp.float32)
    for row_tap in range(3):
        for col_tap in range(3):
            top = margin + (row_tap - 1) * rate
            left = margin + (col_tap - 1) * rate
            window = padded[top : top + height, left : left + width].reshape(height * width, -1)
            summed = summed + jnp.dot(
                window, weights[row_tap, col_tap], preferred_element_type=jnp.float32
            )
    return summed


def left_product(first, second):
    return lax.dot_general(
        first, second, (((0,), (0,)), ((), ())), preferred_element_type=jnp.float32
    )


def right_product(first, second):
    return lax.dot_general(
        first, second, (((1,), (1,)), ((), ())), preferred_element_type=jnp.float32
    )


def atrous_grad(padded, branch_grad, rate, height, width, margin):
    blocks = []
    for row_tap in range(3):
        for col_tap in range(3):
            top = margin + (row_tap - 1) * rate
            left = margin + (col_tap - 1) * rate
            window = padded[top : top + height, left : left + width].reshape(height * width, -1)
            blocks.append(left_product(window, branch_grad))
    return jnp.stack(blocks).reshape(3, 3, blocks[0].shape[0], blocks[0].shape[1])


def head_terms(padded, label_map, w_one, w_atrous, w_proj, w_class, height, width, loss_scale):
    margin = RATE_B
    center = padded[margin : margin + height, margin : margin + width].reshape(height * width, -1)
    pre_list = (
        jnp.dot(center, w_one, preferred_element_type=jnp.float32),
        atrous_sum(padded, w_atrous[0], RATE_A, height, width, margin),
        atrous_sum(padded, w_atrous[1], RATE_B, height, width, margin),
    )
    branch_list = tuple((jax.nn.silu(pre).astype(jnp.bfloat16) for pre in pre_list))
    joined = jnp.concatenate(branch_list, axis=1)
    pre_hidden = jnp.dot(joined, w_proj, preferred_element_type=jnp.float32)
    hidden = jax.nn.silu(pre_hidden).astype(jnp.bfloat16)
    logits = jnp.dot(hidden, w_class, preferred_element_type=jnp.float32)
    log_total = jnp.log(jnp.sum(jnp.exp(logits), axis=1))
    onehot = (
        label_map.reshape(-1)[:, None] == jnp.arange(logits.shape[1], dtype=jnp.int32)[None, :]
    ).astype(jnp.float32)
    loss_sum = jnp.sum(log_total - jnp.sum(onehot * logits, axis=1))
    softmax_probs = jnp.exp(logits - log_total[:, None])
    dlogits = ((softmax_probs - onehot) * loss_scale).astype(jnp.bfloat16)
    grad_class = left_product(hidden, dlogits)
    hidden_grad = (right_product(dlogits, w_class) * silu_slope(pre_hidden)).astype(jnp.bfloat16)
    grad_proj = left_product(joined, hidden_grad)
    joined_grad = right_product(hidden_grad, w_proj)
    out_width = w_proj.shape[1]
    branch_grads = []
    for branch_index in range(3):
        block = joined_grad[:, branch_index * out_width : (branch_index + 1) * out_width]
        branch_grads.append((block * silu_slope(pre_list[branch_index])).astype(jnp.bfloat16))
    grad_one = left_product(center, branch_grads[0])
    grad_atrous = jnp.stack(
        [
            atrous_grad(padded, branch_grads[1], RATE_A, height, width, margin),
            atrous_grad(padded, branch_grads[2], RATE_B, height, width, margin),
        ]
    )
    return (grad_atrous, grad_one, grad_proj, grad_class, loss_sum)


def on_device(features, labels, w_one, w_atrous, w_proj, w_class):
    sample_image = features[0]
    rows_dev = sample_image.shape[0]
    width = sample_image.shape[1]
    near = [from_behind(sample_image, "space", offset) for offset in (1, -1)]
    far_parts = (
        (2, sample_image[2 * rows_dev - RATE_B :]),
        (-2, sample_image[: RATE_B - rows_dev]),
    )
    far = [from_behind(window, "space", offset) for offset, window in far_parts]
    extended = jnp.concatenate([far[0], near[0], sample_image, near[1], far[1]], axis=0)
    padded = jnp.pad(extended, ((0, 0), (RATE_B, RATE_B), (0, 0)))
    total_pix = lax.axis_size("dp") * lax.axis_size("space") * rows_dev * width
    terms = head_terms(
        padded,
        labels[0],
        w_one,
        w_atrous,
        w_proj,
        w_class,
        rows_dev,
        width,
        1.0 / math.sqrt(total_pix),
    )
    local_grad = terms[0]
    grad_atrous = lax.psum_scatter(local_grad, ("dp", "space"), scatter_dimension=3, tiled=True)
    grad_one, grad_proj, grad_class, loss_sum = lax.psum(
        (terms[1], terms[2], terms[3], terms[4]), ("dp", "space")
    )
    return (grad_atrous, grad_one, grad_proj, grad_class, loss_sum / total_pix)


def solution(mesh):
    return jax.shard_map(
        on_device,
        mesh=mesh,
        in_specs=(P("dp", "space", None, None), P("dp", "space", None), P(), P(), P(), P()),
        out_specs=(P(None, None, None, ("dp", "space"), None), P(), P(), P(), P()),
        check_vma=False,
    )
```

profile of v0, /device:TPU:1, one launch (start us, length us, event | category | flops | bytes accessed | tf_op | source)
XLA Modules:
  0.0 512.6 jit_solution(15512943967529032391)
XLA Ops:
  7.2 3.5 collective-permute-start.2
  10.7 3.2 collective-permute-start.1
  13.9 2.5 slice_bitcast_fusion.2
  16.4 1.3 collective-permute-start.3
  17.7 5.8 %collective-permute-start = (bf16[6,56,1024]{2,1,0:T(8,128)(2,1)}, bf16[6,56,1024]{2,1,0:T(8,128)(2,1)}, u32[]{:S(2)}, u32[]{:S(2)}) collective-permute-start(bf16[6,56,1024]{2,1,0:T(8,128)(2,1)} %get-tuple-element.37), channel_id=1, source_target_pairs={{0,2},{1,3},{4,6},{5,7},{8,10},{9,11},{12,14},{13,15},{16,18},{17,... | collective-permute-start | bytes 2064392 | tf_op jit(solution)/shard_map/ppermute | solution.py:15
  23.5 6.8 %slice_bitcast_fusion.1 = (bf16[3,3,1024,256]{3,2,1,0:T(8,128)(2,1)S(1)}, bf16[3,3,1024,256]{3,2,1,0:T(8,128)(2,1)}) fusion(bf16[2,3,3,1024,256]{4,3,2,1,0:T(8,128)(2,1)} %param.9), kind=kLoop, calls=%fused_computation.14 | loop fusion | bytes 18874368 | tf_op jit(solution)/shard_map/squeeze | solution.py:64
  30.3 2.2 copy-done.4
  32.5 1.5 fusion.44
  34.0 2.5 fusion.37
  36.5 1.5 multiply_convert_fusion.3
  38.0 6.2 %collective-permute-done = bf16[6,56,1024]{2,1,0:T(8,128)(2,1)} collective-permute-done((bf16[6,56,1024]{2,1,0:T(8,128)(2,1)}, bf16[6,56,1024]{2,1,0:T(8,128)(2,1)}, u32[]{:S(2)}, u32[]{:S(2)}) %collective-permute-start) | collective-permute-done | bytes 688160 | tf_op jit(solution)/shard_map/ppermute | solution.py:15
  44.2 1.1 constant_dynamic-update-slice_fusion.4
  45.4 1.4 fusion.42
  46.8 2.0 pad_maximum_fusion.2
  48.8 3.3 fusion.47
  52.1 1.4 pad_maximum_fusion.1
  53.6 1.4 fusion.35
  54.9 1.4 fusion.40
  56.3 1.1 constant_dynamic-update-slice_fusion
  57.5 6.6 %pad_slice_fusion.8 = (bf16[12,56,1024]{2,1,0:T(8,128)(2,1)S(1)}, bf16[12,56,1024]{2,1,0:T(8,128)(2,1)}, bf16[12,56,1024]{2,1,0:T(8,128)(2,1)S(1)}, bf16[12,56,1...) fusion(bf16[48,56,1024]{2,1,0:T(8,128)(2,1)S(1)} %constant_dyna, ...), kind=kLoop, calls=%fused_computation.9 | loop fusion | bytes 22020096 | tf_op jit(solution)/shard_map/slice | solution.py:29
  64.2 2.9 fusion.46
  70.9 0.5 copy-done.40
  72.2 0.6 copy-done.46
  72.7 1.5 multiply_convert_fusion.2
  74.8 0.5 copy-done.47
  75.3 1.5 multiply_convert_fusion.1
  77.8 0.6 subtract_reduce_fusion
  78.8 1.4 fusion.48
  80.7 1.3 copy-done.6
  82.0 1.7 convolution_bitcast_fusion
  83.7 2.3 fusion.33
  86.0 0.6 fusion.17
  86.6 2.2 fusion.16
  88.8 0.6 fusion.15
  89.5 0.7 copy-done.36
  90.2 0.6 fusion.14
  90.8 0.7 fusion.13
  91.5 0.6 copy-done.34
  92.1 0.6 fusion.12
  92.8 0.7 copy-done.32
  93.5 0.9 fusion.11
  94.3 0.7 fusion.10
  95.1 0.6 copy-done.30
  95.7 0.6 fusion.9
  96.3 0.7 copy-done.8
  97.0 1.7 fusion.8
  98.7 0.7 copy-done.14
  99.4 1.6 fusion.7
  101.0 0.8 copy-done.28
  101.7 1.6 fusion.6
  103.3 1.6 fusion.5
  104.9 1.7 fusion.4
  106.6 1.6 fusion.3
  108.3 1.6 fusion.2
  109.8 1.6 fusion.1
  111.6 0.9 copy-done.18
  112.9 1.6 fusion
  114.5 14.7 %pad_maximum_fusion = f32[2,3,3,1024,256]{4,3,2,1,0:T(8,128)} fusion(f32[1,3,3,1024,256]{4,3,2,1,0:T(8,128)} %bitcast.63, f32[1,3,3,1024,256]{4,3,2,1,0:T(8,128)} %bitcast.244), kind=kLoop, calls=%fused_computation | loop fusion | flops 4718592 | bytes 37748736 | tf_op jit(solution)/shard_map/stack | solution.py:89
  129.2 1.0 copy-done.16
  130.3 68.8 %all-reduce.1 = (f32[256,3]{0,1:T(4,128)}, f32[]{:T(128)}) all-reduce(f32[256,3]{0,1:T(4,128)S(1)} %fusion.56, f32[]{:T(128)} %get-tuple-element.38), channel_id=1, replica_groups=mesh['dp'=32,'space'=4] {'dp','space'}, use_global_device_ids=true, to_apply=%region_4.5 | all-reduce | flops 769 | bytes 6152 | tf_op jit(solution)/shard_map/psum | solution.py:124
  199.8 64.7 %all-reduce.5.cloned.1.call-done = (f32[1024,256]{0,1:T(8,128)}, f32[768,256]{1,0:T(8,128)}) async-done(((f32[1024,256]{0,1:T(8,128)}, f32[768,256]{1,0:T(8,128)}), (f32[1024,256]{0,1:T(8,128)}, f32[768,256]{1,0:T(8,128)})) %all-reduce.5.cloned.1.call-update) | async-done | bytes 1835024 | tf_op jit(solution)/shard_map/psum | solution.py:124
  264.6 2.6 copy.15
  267.2 236.6 %reduce-scatter.2.cloned.1.call-done = f32[2,3,3,8,256]{4,3,2,1,0:T(8,128)} async-done(((f32[2,3,3,1024,256]{4,3,2,1,0:T(8,128)}), f32[2,3,3,8,256]{4,3,2,1,0:T(8,128)}) %reduce-scatter.2.cloned.1.call-update) | async-done | bytes 147472 | tf_op jit(solution)/shard_map/reduce_scatter | solution.py:123
  503.8 0.9 copy.42
  (116 shorter events, 7.8 us)
Async XLA Ops:
  7.2 29.3 %copy-start = (bf16[1024,256]{1,0:T(8,128)(2,1)S(1)}, bf16[1024,256]{1,0:T(8,128)(2,1)}, u32[]{:S(2)}) copy-start(bf16[1024,256]{1,0:T(8,128)(2,1)} %param.8) | copy-start | bytes 1572868
  7.2 257.4 %all-reduce.5.cloned.1.call-start = ((), (), s32[]{:S(2)}) async-start(), calls=%async_computation.2 | async-start | bytes 3670016 | tf_op jit(solution)/shard_map/psum | solution.py:124
  7.2 38.1 %collective-permute-start.2 = (bf16[12,56,1024]{2,1,0:T(8,128)(2,1)}, bf16[12,56,1024]{2,1,0:T(8,128)(2,1)S(1)}, u32[]{:S(2)}, u32[]{:S(2)}) collective-permute-start(bf16[12,56,1024]{2,1,0:T(8,128)(2,1)} %bitcast.236), channel_id=1, source_target_pairs={{1,0},{2,1},{3,2},{5,4},{6,5},{7,6},{9,8},{10,9},{11,10},{13,12},{... | collective-permute-start | bytes 4128776 | tf_op jit(solution)/shard_map/ppermute | solution.py:15
  10.7 36.1 %collective-permute-start.1 = (bf16[12,56,1024]{2,1,0:T(8,128)(2,1)}, bf16[12,56,1024]{2,1,0:T(8,128)(2,1)}, u32[]{:S(2)}, u32[]{:S(2)}) collective-permute-start(bf16[12,56,1024]{2,1,0:T(8,128)(2,1)} %bitcast.237), channel_id=1, source_target_pairs={{0,1},{1,2},{2,3},{4,5},{5,6},{6,7},{8,9},{9,10},{10,11},{12,13},{... | collective-permute-start | bytes 4128776 | tf_op jit(solution)/shard_map/ppermute | solution.py:15
  16.4 35.8 %collective-permute-start.3 = (bf16[6,56,1024]{2,1,0:T(8,128)(2,1)}, bf16[6,56,1024]{2,1,0:T(8,128)(2,1)}, u32[]{:S(2)}, u32[]{:S(2)}) collective-permute-start(bf16[6,56,1024]{2,1,0:T(8,128)(2,1)} %get-tuple-element.36), channel_id=1, source_target_pairs={{2,0},{3,1},{6,4},{7,5},{10,8},{11,9},{14,12},{15,13},{18,16},{19,... | collective-permute-start | bytes 2064392 | tf_op jit(solution)/shard_map/ppermute | solution.py:15
  17.7 14.8 %copy-start.2 = (bf16[1,12,56,1024]{3,2,1,0:T(8,128)(2,1)S(1)}, bf16[1,12,56,1024]{3,2,1,0:T(8,128)(2,1)}, u32[]{:S(2)}) copy-start(bf16[1,12,56,1024]{3,2,1,0:T(8,128)(2,1)} %param.6) | copy-start | bytes 4128772
  17.7 26.5 %collective-permute-start = (bf16[6,56,1024]{2,1,0:T(8,128)(2,1)}, bf16[6,56,1024]{2,1,0:T(8,128)(2,1)}, u32[]{:S(2)}, u32[]{:S(2)}) collective-permute-start(bf16[6,56,1024]{2,1,0:T(8,128)(2,1)} %get-tuple-element.37), channel_id=1, source_target_pairs={{0,2},{1,3},{4,6},{5,7},{8,10},{9,11},{12,14},{13,15},{16,18},{17,... | collective-permute-start | bytes 2064392 | tf_op jit(solution)/shard_map/ppermute | solution.py:15
  30.3 2.2 copy-start.4
  30.3 3.6 copy-start.44
  36.5 8.9 %copy-start.5 = (bf16[3,3,1024,256]{3,2,1,0:T(8,128)(2,1)S(1)}, bf16[3,3,1024,256]{3,2,1,0:T(8,128)(2,1)}, u32[]{:S(2)}) copy-start(bf16[3,3,1024,256]{3,2,1,0:T(8,128)(2,1)} %copy-done.4) | copy-start | bytes 14155780
  48.7 6.2 %copy-start.13 = (bf16[12,56,1024]{2,1,0:T(8,128)(2,1)}, bf16[12,56,1024]{2,1,0:T(8,128)(2,1)S(1)}, u32[]{:S(2)}) copy-start(bf16[12,56,1024]{2,1,0:T(8,128)(2,1)S(1)} %get-tuple-element.32) | copy-start | bytes 4128772
  48.7 4.8 slice-start
  52.0 1.5 slice-start.1
  53.5 2.8 copy-start.11
  64.1 4.6 copy-start.29
  64.1 4.6 copy-start.31
  64.1 4.6 copy-start.35
  64.1 4.6 copy-start.27
  64.1 5.1 %copy-start.25 = (bf16[12,56,1024]{2,1,0:T(8,128)(2,1)}, bf16[12,56,1024]{2,1,0:T(8,128)(2,1)S(1)}, u32[]{:S(2)}) copy-start(bf16[12,56,1024]{2,1,0:T(8,128)(2,1)S(1)} %get-tuple-element.25) | copy-start | bytes 4128772
  64.1 5.7 %copy-start.21 = (bf16[12,56,1024]{2,1,0:T(8,128)(2,1)}, bf16[12,56,1024]{2,1,0:T(8,128)(2,1)S(1)}, u32[]{:S(2)}) copy-start(bf16[12,56,1024]{2,1,0:T(8,128)(2,1)S(1)} %get-tuple-element.27) | copy-start | bytes 4128772
  64.1 6.2 %copy-start.19 = (bf16[12,56,1024]{2,1,0:T(8,128)(2,1)}, bf16[12,56,1024]{2,1,0:T(8,128)(2,1)S(1)}, u32[]{:S(2)}) copy-start(bf16[12,56,1024]{2,1,0:T(8,128)(2,1)S(1)} %get-tuple-element.28) | copy-start | bytes 4128772
  64.1 6.7 %copy-start.9 = (bf16[12,56,1024]{2,1,0:T(8,128)(2,1)}, bf16[12,56,1024]{2,1,0:T(8,128)(2,1)S(1)}, u32[]{:S(2)}) copy-start(bf16[12,56,1024]{2,1,0:T(8,128)(2,1)S(1)} %get-tuple-element.29) | copy-start | bytes 4128772
  64.2 8.0 %copy-start.33 = (bf16[12,56,1024]{2,1,0:T(8,128)(2,1)}, bf16[12,56,1024]{2,1,0:T(8,128)(2,1)S(1)}, u32[]{:S(2)}) copy-start(bf16[12,56,1024]{2,1,0:T(8,128)(2,1)S(1)} %get-tuple-element.18) | copy-start | bytes 4128772
  64.2 10.0 %copy-start.7 = (bf16[12,56,1024]{2,1,0:T(8,128)(2,1)}, bf16[12,56,1024]{2,1,0:T(8,128)(2,1)S(1)}, u32[]{:S(2)}) copy-start(bf16[12,56,1024]{2,1,0:T(8,128)(2,1)S(1)} %get-tuple-element.23) | copy-start | bytes 4128772
  64.2 10.6 %copy-start.23 = (bf16[12,56,1024]{2,1,0:T(8,128)(2,1)}, bf16[12,56,1024]{2,1,0:T(8,128)(2,1)S(1)}, u32[]{:S(2)}) copy-start(bf16[12,56,1024]{2,1,0:T(8,128)(2,1)S(1)} %get-tuple-element.26) | copy-start | bytes 4128772
  70.3 1.1 copy-start.40
  70.3 1.3 copy-start.41
  71.6 1.1 copy-start.46
  72.7 1.5 copy-start.39
  72.7 1.5 copy-start.42
  74.2 1.1 copy-start.47
  75.3 1.5 copy-start.43
  75.3 1.5 copy-start.49
  76.9 0.7 copy-start.45
  77.3 1.5 copy-start.15
  80.2 1.8 copy-start.48
  80.6 1.3 copy-start.6
  83.7 2.3 copy-start.10
  86.0 23.9 %copy-start.17 = (bf16[672,256]{1,0:T(8,128)(2,1)}, bf16[672,256]{1,0:T(8,128)(2,1)S(1)}, u32[]{:S(2)}) copy-start(bf16[672,256]{1,0:T(8,128)(2,1)S(1)} %get-tuple-element.31) | copy-start | bytes 1032196
  86.6 2.2 copy-start.37
  88.8 1.3 copy-start.36
  90.8 1.3 copy-start.34
  92.1 1.3 copy-start.32
  94.3 1.3 copy-start.30
  95.7 1.3 copy-start.8
  96.3 7.0 %copy-start.3 = (f32[9,1024,256]{2,1,0:T(8,128)}, f32[9,1024,256]{2,1,0:T(8,128)S(1)}, u32[]{:S(2)}) copy-start(f32[9,1024,256]{2,1,0:T(8,128)S(1)} %fusion.9) | copy-start | bytes 28311556
  97.0 2.3 copy-start.14
  99.4 2.4 copy-start.28
  101.7 1.6 copy-start.26
  104.9 1.7 copy-start.24
  106.6 1.6 copy-start.22
  108.3 1.6 copy-start.12
  111.5 1.0 copy-start.18
  111.5 1.5 copy-start.20
  111.5 392.2 %reduce-scatter.2.cloned.1.call-start = ((), (), s32[]{:S(2)}) async-start(), calls=%async_computation.1 | async-start | bytes 19021824 | tf_op jit(solution)/shard_map/reduce_scatter | solution.py:123
  129.2 1.0 copy-start.16
  264.5 239.2 %copy-start.38 = (f32[768,256]{1,0:T(8,128)S(1)}, f32[768,256]{1,0:T(8,128)}, u32[]{:S(2)}) copy-start(f32[768,256]{1,0:T(8,128)} %get-tuple-element.51) | copy-start | bytes 2359300
  264.5 240.1 %copy-start.1 = (bf16[1024,256]{1,0:T(8,128)(2,1)S(1)}, bf16[1024,256]{1,0:T(8,128)(2,1)}, u32[]{:S(2)}) copy-start(bf16[1024,256]{1,0:T(8,128)(2,1)} %param.8) | copy-start | bytes 1572868
Sparse Core Ops, SparseCore 0:
  111.6 152.8 all-reduce.4
  270.4 233.3 reduce-scatter.1
where the time goes:
time: 515 us; the launch traced here: 513 us
  waiting for transfers between devices  308 us (60%)
  blocking collectives  68.8 us (13%)
  matrix products  50.3 us (10%)
  local copies, waits for them, and re-layouts  34.7 us (7%)
  other arithmetic  21 us (4%)
  between operations  16.4 us (3%)
  starting transfers between devices  13.8 us (3%)
    reduce_scatter x1, waiting for transfers between devices, on_device(): lax.psum_scatter(local_grad, ('dp', 'space'), scatter_dimension=3, tiled=...  237 us
    psum x1, blocking collectives, on_device(): lax.psum((terms[1], terms[2], terms[3], terms[4]), ('dp', 'space'))  68.8 us
    psum x1, waiting for transfers between devices, on_device(): lax.psum((terms[1], terms[2], terms[3], terms[4]), ('dp', 'space'))  64.7 us
    dot_general x21, matrix products, left_product(): lax.dot_general(first, second, (((0,), (0,)), ((), ())), preferred_elemen...  25.4 us
    dot_general x18, matrix products, atrous_sum(): jnp.dot(window, weights[row_tap, col_tap], preferred_element_type=jnp.flo...  21.9 us
    unnamed x108, local copies, waits for them, and re-layouts  17.6 us
    another operation x1, other arithmetic, head_terms(): jnp.stack([atrous_grad(padded, branch_grads[1], RATE_A, height, width, ma...  14.7 us
    ppermute x4, starting transfers between devices, from_behind(): lax.ppermute(value, axis, [(source, source + steps) for source in range(f...  13.8 us
  transfers between devices with their start and end apart: 6, of which 3 were waited for; matrix products, arithmetic and copies ran while one was open for 8% of the time, Pallas kernels for 0%

commit v1 on v0

v1 whole, which is shorter than its diff:
```python
import math

import jax
import jax.numpy as jnp
from jax import lax
from jax.experimental import pallas as pl
from jax.experimental.pallas import tpu as pltpu
from jax.sharding import PartitionSpec as P

MESH = pl.DeviceIdType.MESH
BF = jnp.bfloat16
F32 = jnp.float32
WIDTH = 56
BLK = 6 * WIDTH
OWN = 12 * WIDTH
CHIP = 24 * WIDTH
BASE = 3
ORDERS = ("xzy", "zyx", "yxz", "zxy")
AXES = "xzy"


def slope(pre):
    gate = jax.nn.sigmoid(pre)
    return gate * (1.0 + pre * (1.0 - gate))


def silu(pre):
    return pre * jax.nn.sigmoid(pre)


def mm(first, second):
    return jnp.dot(first, second, preferred_element_type=F32)


def mm_t(first, second):
    return lax.dot_general(first, second, (((1,), (1,)), ((), ())), preferred_element_type=F32)


def t_mm(first, second):
    return lax.dot_general(first, second, (((0,), (0,)), ((), ())), preferred_element_type=F32)


def kernel(
    loss_scale,
    feat, labels, w_one_h, w_atr_h, w_proj, w_cls,
    o_atr, o_one, o_proj, o_cls,
    xbuf, xt, wbuf, wone, tacc, pre, pre0, cs, cr, joined, dh, ext, db0, raw, hraw,
    s1, r1, s2, r2, s3, r3, fin, pbuf, e1, eout, eoth, clbuf, swap,
    lsem, ssem, rsem,
):
    dp = lax.axis_index("dp")
    sp = lax.axis_index("space")
    core, s = sp % 2, sp // 2
    cx, cz, cy = dp // 8, (dp // 2) % 4, (dp % 2) * 2 + s
    here = {"x": cx, "z": cz, "y": cy}

    def place(x, z, y, c):
        return (x * 8 + z * 2 + y // 2, (y % 2) * 2 + c)

    partner = place(cx, cz, cy, 1 - core)
    across = (dp, (1 - s) * 2 + core)

    def peer(axis, d):
        at = dict(here)
        at[axis] = (at[axis] + d) % 4
        return place(at["x"], at["z"], at["y"], core)

    rate = 12 + 6 * core
    k = 2 + core

    counter = [0]

    def remote(src, dst, to):
        i = counter[0]
        counter[0] += 1
        return pltpu.make_async_remote_copy(
            src_ref=src, dst_ref=dst, send_sem=ssem.at[i], recv_sem=rsem.at[i], device_id=to, device_id_type=MESH
        )

    sends = []

    def go(copy):
        copy.start()
        sends.append(copy)
        return copy

    own_rows = pl.ds(pl.multiple_of(core * OWN, 16), OWN)
    other_rows = pl.ds(pl.multiple_of((1 - core) * OWN, 16), OWN)
    x_local = pltpu.make_async_copy(feat, xbuf.at[own_rows], lsem.at[0])
    x_local.start()
    w_local = [pltpu.make_async_copy(w_atr_h.at[core, a], wbuf.at[a], lsem.at[1 + a]) for a in range(3)]
    for copy in w_local:
        copy.start()
    one_local = pltpu.make_async_copy(w_one_h, wone, lsem.at[4])
    one_local.start()

    barrier = pltpu.get_barrier_semaphore()
    greet = [partner] + [peer(axis, d) for axis in AXES for d in (1, 2, 3)]
    for other in greet:
        pl.semaphore_signal(barrier, inc=1, device_id=other, device_id_type=MESH)
    pl.semaphore_wait(barrier, len(greet))

    x_swap = go(remote(feat, xbuf.at[own_rows], partner))

    zero = jnp.zeros((BLK, 256), BF)
    for b in range(3):
        for m in (0, 1, 2, 7, 8, 9):
            ext[b, pl.ds(m * BLK, BLK), :] = zero

    column = lax.rem(lax.broadcasted_iota(jnp.int32, (BLK, 256), 0), WIDTH)

    def from_left(value):
        return jnp.where(column >= rate, pltpu.roll(value, rate, 0), 0.0)

    def from_right(value):
        return jnp.where(column < WIDTH - rate, pltpu.roll(value, BLK - rate, 0), 0.0)

    def block(m):
        return pl.ds(pl.multiple_of(m * BLK, 16), BLK)

    x_local.wait()
    x_swap.wait_recv()
    for copy in w_local:
        copy.wait()
    cross_tap = s * 2
    cross_copies = [remote(cs.at[t], cr.at[t], across) for t in range(3)]
    for t in range(3):
        @pl.when(t < k)
        def _(t=t):
            src = jnp.where(s == 0, 4 + t - k, t)
            rows = xbuf[block(src), :]
            parts = [mm(rows, wbuf[cross_tap, b]) for b in range(3)]
            cs[t] = (parts[1] + from_left(parts[0]) + from_right(parts[2])).astype(BF)
            cross_copies[t].start()

    @pl.loop(0, 4)
    def _(i):
        rows = xbuf[block(i), :]
        for b in range(3):
            tacc[b] = mm(rows, wbuf[1, b])
        for a in (0, 2):
            src = i + (a - 1) * k

            @pl.when((src >= 0) & (src < 4))
            def _(a=a, src=src):
                shifted = xbuf[block(src), :]
                for b in range(3):
                    tacc[b] += mm(shifted, wbuf[a, b])
        pre[block(i), :] = tacc[1] + from_left(tacc[0]) + from_right(tacc[2])

    one_local.wait()

    @pl.when(core == 1)
    def _():
        @pl.loop(0, 4)
        def _(i):
            value = mm(xbuf[block(i), :], wone[...])
            pre0[block(i), :] = value
            joined[0, block(i), :] = silu(value).astype(BF)

    for t in range(3):
        @pl.when(t < k)
        def _(t=t):
            cross_copies[t].wait_recv()
            into = block(jnp.where(s == 0, 4 - k + t, t))
            pre[into, :] += cr[t].astype(F32)

    @pl.loop(0, 4)
    def _(i):
        joined[1 + core, block(i), :] = silu(pre[block(i), :]).astype(BF)

    j_copies = [remote(joined.at[b, other_rows], joined.at[b, other_rows], partner) for b in range(3)]

    @pl.when(core == 0)
    def _():
        j_copies[1].start()

    @pl.when(core == 1)
    def _():
        j_copies[0].start()
        j_copies[2].start()

    for c in range(4):
        xt[c] = xbuf[:, c * 256 : (c + 1) * 256].T

    @pl.when(core == 0)
    def _():
        j_copies[0].wait_recv()
        j_copies[2].wait_recv()

    @pl.when(core == 1)
    def _():
        j_copies[1].wait_recv()

    pre_hidden = mm(joined[0, own_rows, :], w_proj[0])
    pre_hidden += mm(joined[1, own_rows, :], w_proj[1])
    pre_hidden += mm(joined[2, own_rows, :], w_proj[2])
    hidden = silu(pre_hidden).astype(BF)
    logits = mm_t(w_cls[...], hidden)
    row = lax.broadcasted_iota(jnp.int32, logits.shape, 0)
    valid = row < 3
    top = jnp.max(jnp.where(valid, logits, -jnp.inf), axis=0, keepdims=True)
    total = jnp.sum(jnp.where(valid, jnp.exp(logits - top), 0.0), axis=0, keepdims=True)
    lse = top + jnp.log(total)
    onehot = row == labels[...]
    loss = jnp.sum(lse - jnp.sum(jnp.where(onehot, logits, 0.0), axis=0, keepdims=True), axis=1, keepdims=True)
    probs = jnp.exp(logits - lse) - jnp.where(onehot, 1.0, 0.0)
    dlogits = jnp.where(valid, probs * loss_scale, 0.0).astype(BF)
    dhidden = t_mm(dlogits, w_cls[...]) * slope(pre_hidden)
    dh[own_rows, :] = dhidden.astype(BF)
    dh_copy = go(remote(dh.at[own_rows], dh.at[own_rows], partner))

    small = mm(dlogits, hidden)
    srow = lax.broadcasted_iota(jnp.int32, small.shape, 0)
    cl_copies = []
    for n, axis in enumerate(AXES):
        cl_copies.append([remote(clbuf.at[n, here[axis]], clbuf.at[n, here[axis]], peer(axis, d)) for d in (1, 2, 3)])
    cl_copies.append([remote(clbuf.at[3, core], clbuf.at[3, core], partner)])
    clbuf[0, here["x"]] = jnp.where(srow == 3, loss, small)
    for copy in cl_copies[0]:
        go(copy)

    def small_step(n):
        for copy in cl_copies[n]:
            copy.wait_recv()
        value = clbuf[n, 0] + clbuf[n, 1]
        if n < 3:
            value = value + clbuf[n, 2] + clbuf[n, 3]
            clbuf[n + 1, core if n == 2 else here[AXES[n + 1]]] = value
            for copy in cl_copies[n + 1]:
                go(copy)
        else:
            o_cls[...] = value

    dh_copy.wait_recv()
    branch_w = w_proj[1 + core]
    raw_copies = [remote(raw.at[block(jnp.where(s == 0, 4 - k + t, t))], hraw.at[t], across) for t in range(3)]

    @pl.loop(0, 4)
    def _(i):
        value = mm_t(dh[block(i), :], branch_w) * slope(pre[block(i), :])
        raw[block(i), :] = value.astype(BF)
        to = block(BASE + i)
        rounded = value.astype(BF).astype(F32)
        ext[0, to, :] = from_right(rounded).astype(BF)
        ext[1, to, :] = rounded.astype(BF)
        ext[2, to, :] = from_left(rounded).astype(BF)

    for t in range(3):
        @pl.when(t < k)
        def _(t=t):
            raw_copies[t].start()

    def three(p, phase, buf, landing):
        axis = ORDERS[p][phase]
        left = [a for a in AXES if a in ORDERS[p][phase:]]
        spot = left.index(axis)

        def chunk(at):
            return buf.at[(slice(None),) * (1 + spot) + (at,)]

        return [remote(chunk((here[axis] + d) % 4), landing.at[d - 1], peer(axis, d)) for d in (1, 2, 3)], chunk(here[axis])

    plans = []
    for p in range(4):
        taps = 3 if p < 3 else 1
        sl = slice(3 * p, 3 * p + 3) if p < 3 else slice(9, 10)
        first = s1.at[p] if p < 3 else e1
        lead = pl.ds(sl.start, taps)
        bufs = (first, s2.at[lead], s3.at[lead])
        lands = (r1.at[:, lead], r2.at[:, lead], r3.at[:, lead])
        plan = []
        for phase in range(3):
            copies, mine = three(p, phase, bufs[phase], lands[phase])
            plan.append((copies, mine, lands[phase]))
        plans.append((plan, bufs, taps, lead))

    def send(p, phase):
        for copy in plans[p][0][phase][0]:
            go(copy)

    def settle(p, phase):
        plan, bufs, taps, lead = plans[p]
        copies, mine, landing = plan[phase]
        for copy in copies:
            copy.wait_recv()

        def one(t):
            value = mine[t].astype(F32)
            for d in range(3):
                value = value + landing[d, t].astype(F32)
            if phase < 2:
                bufs[phase + 1][t] = value.astype(BF)
            else:
                fin[lead.start + t] = value

        if taps == 1:
            one(0)
        else:
            pl.loop(0, taps)(one)
        if phase < 2:
            send(p, phase + 1)

    def proj_grad(b):
        return t_mm(joined[b], dh[...]).astype(BF).reshape(4, 4, 16, 256)

    p_copies = [remote(pbuf.at[n], e1.at[0, 2 * n], partner) for n in range(2)]

    @pl.when(core == 1)
    def _():
        for n in range(2):
            pbuf[n] = proj_grad(2 * n)
            p_copies[n].start()

        @pl.loop(0, 4)
        def _(i):
            value = mm_t(dh[block(i), :], w_proj[0]) * slope(pre0[block(i), :])
            db0[block(i), :] = value.astype(BF)

        @pl.loop(0, 4)
        def _(c):
            e1[0, c] = mm(xt[c], db0[...]).astype(BF).reshape(4, 4, 16, 256)

    @pl.when(core == 0)
    def _():
        e1[0, 1] = proj_grad(1)
        e1[0, 3] = jnp.zeros((4, 4, 16, 256), BF)
        for n in range(2):
            p_copies[n].wait_recv()

    send(3, 0)

    def part(a):
        p = jnp.where(a == 1, 0, 1 + a // 2)
        start = pl.ds(pl.multiple_of((BASE - (a - 1) * k) * BLK, 16), CHIP)

        @pl.loop(0, 4)
        def _(c):
            for b in range(3):
                s1[p, b, c] = mm(xt[c], ext[b, start, :]).astype(BF).reshape(4, 4, 16, 256)

    def outer_send(toward):
        for p in (1, 2):
            @pl.when((s == p - 1) == toward)
            def _(p=p):
                for copy in plans[p][0][0][0]:
                    copy.start()

    part(1)
    send(0, 0)
    small_step(0)
    part(2 - cross_tap)
    outer_send(False)
    settle(3, 0)

    for t in range(3):
        @pl.when(t < k)
        def _(t=t):
            raw_copies[t].wait_recv()
            to = block(jnp.where(s == 0, BASE + 4 + t, BASE - k + t))
            value = hraw[t].astype(F32)
            ext[0, to, :] = from_right(value).astype(BF)
            ext[1, to, :] = hraw[t]
            ext[2, to, :] = from_left(value).astype(BF)

    part(cross_tap)
    outer_send(True)
    for p in (1, 2):
        sends.extend(plans[p][0][0][0])
    small_step(1)
    settle(3, 1)
    settle(0, 0)
    settle(3, 2)

    spots = {"x": cx, "z": cz, "y": cy}
    eout[cx, cz, cy] = fin[9].astype(BF)

    def gather(phase):
        axis = ORDERS[3][phase]
        done = ORDERS[3][phase + 1 :]
        at = tuple(slice(None) if a in done else spots[a] for a in AXES)
        return [remote(eout.at[at], eout.at[at], peer(axis, d)) for d in (1, 2, 3)]

    gathers = [gather(phase) for phase in range(3)]
    for copy in gathers[2]:
        go(copy)
    small_step(2)
    settle(1, 0)
    for copy in gathers[2]:
        copy.wait_recv()
    for copy in gathers[1]:
        go(copy)
    settle(2, 0)
    for copy in gathers[1]:
        copy.wait_recv()
    for copy in gathers[0]:
        go(copy)
    settle(0, 1)
    small_step(3)
    settle(1, 1)
    settle(2, 1)
    for copy in gathers[0]:
        copy.wait_recv()
    e_swap = go(remote(eout, eoth, partner))
    settle(0, 2)
    settle(1, 2)
    settle(2, 2)

    give = pl.ds(pl.multiple_of((1 - core) * 8, 8), 8)
    keep = pl.ds(pl.multiple_of(core * 8, 8), 8)
    swap[0] = fin[0:9, give, :]
    f_swap = go(remote(swap.at[0], swap.at[1], partner))

    e_swap.wait_recv()

    @pl.when(core == 0)
    def _():
        o_proj[...] = eout[0:3].astype(F32).reshape(768, 256)
        o_one[...] = eoth[...].astype(F32).reshape(1024, 256)

    @pl.when(core == 1)
    def _():
        o_proj[...] = eoth[0:3].astype(F32).reshape(768, 256)
        o_one[...] = eout[...].astype(F32).reshape(1024, 256)

    f_swap.wait_recv()
    for p, a in ((0, 1), (1, 0), (2, 2)):
        for b in range(3):
            o_atr[core, a * 3 + b] = fin[3 * p + b, keep, :]
            o_atr[1 - core, a * 3 + b] = swap[1, 3 * p + b]

    for copies in (cross_copies, raw_copies):
        for t in range(3):
            @pl.when(t < k)
            def _(copy=copies[t]):
                copy.wait_send()

    @pl.when(core == 0)
    def _():
        j_copies[1].wait_send()

    @pl.when(core == 1)
    def _():
        for copy in (j_copies[0], j_copies[2], p_copies[0], p_copies[1]):
            copy.wait_send()

    for copy in sends:
        copy.wait_send()
    assert counter[0] <= COPIES


COPIES = 80


def on_device(features, labels, w_one, w_atrous, w_proj, w_class):
    total_pix = lax.axis_size("dp") * lax.axis_size("space") * OWN
    vmem = pl.BlockSpec(memory_space=pltpu.VMEM)
    hbm = pl.BlockSpec(memory_space=pl.ANY)
    scratch = [
        ((CHIP, 1024), BF),
        ((4, 256, CHIP), BF),
        ((3, 3, 1024, 256), BF),
        ((1024, 256), BF),
        ((3, BLK, 256), F32),
        ((CHIP, 256), F32),
        ((CHIP, 256), F32),
        ((3, BLK, 256), BF),
        ((3, BLK, 256), BF),
        ((3, CHIP, 256), BF),
        ((CHIP, 256), BF),
        ((3, 10 * BLK, 256), BF),
        ((CHIP, 256), BF),
        ((CHIP, 256), BF),
        ((3, BLK, 256), BF),
        ((3, 3, 4, 4, 4, 16, 256), BF),
        ((3, 10, 4, 4, 16, 256), BF),
        ((10, 4, 4, 16, 256), BF),
        ((3, 10, 4, 16, 256), BF),
        ((10, 4, 16, 256), BF),
        ((3, 10, 16, 256), BF),
        ((10, 16, 256), F32),
        ((2, 4, 4, 16, 256), BF),
        ((1, 4, 4, 4, 16, 256), BF),
        ((4, 4, 4, 16, 256), BF),
        ((4, 4, 4, 16, 256), BF),
        ((4, 4, 16, 256), F32),
        ((2, 9, 8, 256), F32),
    ]
    w_cls = jnp.pad(w_class.T, ((0, 13), (0, 0)))
    out = pl.pallas_call(
        lambda *refs: kernel(1.0 / math.sqrt(total_pix), *refs),
        out_shape=(
            jax.ShapeDtypeStruct((2, 9, 8, 256), F32),
            jax.ShapeDtypeStruct((1024, 256), F32),
            jax.ShapeDtypeStruct((768, 256), F32),
            jax.ShapeDtypeStruct((16, 256), F32),
        ),
        in_specs=[hbm, vmem, hbm, hbm, vmem, vmem],
        out_specs=(vmem, vmem, vmem, vmem),
        scratch_shapes=[pltpu.VMEM(shape, kind) for shape, kind in scratch]
        + [
            pltpu.SemaphoreType.DMA((5,)),
            pltpu.SemaphoreType.DMA((COPIES,)),
            pltpu.SemaphoreType.DMA((COPIES,)),
        ],
        compiler_params=pltpu.CompilerParams(
            collective_id=0, has_side_effects=True, vmem_limit_bytes=60 * 1024 * 1024
        ),
        name="aspp",
    )(
        features.reshape(OWN, 1024),
        labels.reshape(1, OWN),
        w_one,
        w_atrous,
        w_proj.reshape(3, 256, 256),
        w_cls,
    )
    return (
        out[0].reshape(2, 3, 3, 8, 256),
        out[1],
        out[2],
        out[3][:3].T,
        out[3][3, 0] / total_pix,
    )


def solution(mesh):
    return jax.shard_map(
        on_device,
        mesh=mesh,
        in_specs=(P("dp", "space", None, None), P("dp", "space", None), P(), P(), P(), P()),
        out_specs=(P(None, None, None, ("dp", "space"), None), P(), P(), P(), P()),
        check_vma=False,
    )
```

time: 515 us -> 102 us (0.20)
  waiting for transfers between devices: 308 us -> 0 us
  Pallas kernels: 0 us -> 87.7 us
  blocking collectives: 68.8 us -> 0 us
  matrix products: 50.3 us -> 0 us
  local copies, waits for them, and re-layouts: 34.7 us -> 10.3 us
  other arithmetic: 21 us -> 0.72 us
  between operations: 16.4 us -> 2.43 us
  starting transfers between devices: 13.8 us -> 0 us
    reduce_scatter x1 -> x0, waiting for transfers between devices: 237 us -> none  [on_device(): lax.psum_scatter(local_grad, ('dp', 'space'), scatter_dimension=3, tiled=...]
    pallas_call x0 -> x1, Pallas kernels: none -> 87.7 us  [on_device(): pl.pallas_call(lambda *refs: kernel(1.0 / math.sqrt(total_pix), *refs), o...]
    psum x1 -> x0, blocking collectives: 68.8 us -> none  [on_device(): lax.psum((terms[1], terms[2], terms[3], terms[4]), ('dp', 'space'))]
    psum x1 -> x0, waiting for transfers between devices: 64.7 us -> none  [on_device(): lax.psum((terms[1], terms[2], terms[3], terms[4]), ('dp', 'space'))]
    dot_general x44 -> x0, matrix products: 50.3 us -> none  [the longest x21 25.4 us: left_product(): lax.dot_general(first, second, (((0,), (0,)), ((), ())), preferred_elemen...]
    another operation x1 -> x0, other arithmetic: 14.7 us -> none  [head_terms(): jnp.stack([atrous_grad(padded, branch_grads[1], RATE_A, height, width, ma...]
    ppermute x4 -> x0, starting transfers between devices: 13.8 us -> none  [from_behind(): lax.ppermute(value, axis, [(source, source + steps) for source in range(f...]
    unnamed x108 -> x3, local copies, waits for them, and re-layouts: 17.6 us -> 5.9 us
  transfers between devices with their start and end apart: 6 -> 0, of which waited for: 3 -> 0; matrix products, arithmetic and copies ran while one was open for 8% -> 0% of each run, Pallas kernels for 0% -> 0%
where the time goes in v1:
time: 102 us; the launch traced here: 101 us
  Pallas kernels  87.7 us (86%)
  local copies, waits for them, and re-layouts  10.3 us (10%)
  between operations  2.43 us (2%)
    pallas_call x1, Pallas kernels, on_device(): pl.pallas_call(lambda *refs: kernel(1.0 / math.sqrt(total_pix), *refs), o...  87.7 us
    unnamed x3, local copies, waits for them, and re-layouts  5.9 us

profile of v1, /device:TPU:1, one launch (start us, length us, event | category | flops | bytes accessed | tf_op | source)
XLA Modules:
  0.0 101.2 jit_solution(17080110989230611731)
XLA Ops:
  0.6 0.7 reduce
  1.3 0.7 reshape.25.refs_1_
  2.0 1.3 %pad.4.refs_5_ = bf16[16,256]{1,0:T(8,128)(2,1)} pad(bf16[3,256]{1,0:T(4,128)(2,1)} %bitcast.10, bf16[]{:T(256)} %constant.5.clone.1), padding=0_13x0_0 | pad | bytes 9730 | tf_op jit(solution)/shard_map/jit(_pad)/pad | solution.py:489
  3.3 87.7 %aspp.1 = (f32[2,9,8,256]{3,2,1,0:T(8,128)}, f32[1024,256]{1,0:T(8,128)}, f32[768,256]{1,0:T(8,128)}, f32[16,256]{1,0:T(8,128)}) custom-call(bf16[672,1024]{1,0:T(8,128)(2,1)} %bitcast.7, s32[1,672]{1,0:T(1,128)} %reshape.25.refs_1_, bf16[1024,256]{1,0:T(8,128)(2,1)} %refs_2_.1, bf16[2,3,3,1024,256]{4,3,2,1,0:T(8,128)(2,1)} %refs_3_.1, ...), custom_call_target="tpu_custom_call" | custom-call | tf_op jit(solution)/shard_map/aspp/pallas_call | solution.py:490
  91.0 1.2 %slice.7 = f32[1,1]{1,0:T(1,128)} slice(f32[16,256]{1,0:T(8,128)} %get-tuple-element.12), slice={[3:4], [0:1]} | slice | bytes 8 | tf_op jit(solution)/shard_map/slice | solution.py:523
  92.9 1.3 %slice_bitcast_fusion = f32[256,3]{0,1:T(4,128)} fusion(f32[16,256]{1,0:T(8,128)} %get-tuple-element.12), kind=kLoop, calls=%fused_computation | loop fusion | bytes 6144 | tf_op jit(solution)/shard_map/transpose | solution.py:522
  94.1 1.6 %copy.14 = f32[2,3,3,8,256]{4,3,2,1,0:T(8,128)} copy(f32[2,3,3,8,256]{4,3,2,1,0:T(8,128)} %bitcast.9) | data formatting | bytes 294912
  95.7 2.3 %copy.15 = f32[1024,256]{1,0:T(8,128)} copy(f32[1024,256]{1,0:T(8,128)} %get-tuple-element.19) | data formatting | bytes 2097152
  98.0 2.1 %copy.16 = f32[768,256]{1,0:T(8,128)} copy(f32[768,256]{1,0:T(8,128)} %get-tuple-element.20) | data formatting | bytes 1572864

commit v2 on v1

--- a/solution.py
+++ b/solution.py
@@ -43,9 +43,9 @@
 def kernel(
     loss_scale,
     feat, labels, w_one_h, w_atr_h, w_proj, w_cls,
-    o_atr, o_one, o_proj, o_cls,
+    o_atr, eout, o_cls,
     xbuf, xt, wbuf, wone, tacc, pre, pre0, cs, cr, joined, dh, ext, db0, raw, hraw,
-    s1, r1, s2, r2, s3, r3, fin, pbuf, e1, eout, eoth, clbuf, swap,
+    s1, r1, s2, r2, s3, r3, fin, pbuf, e1, clbuf, swap, lab,
     lsem, ssem, rsem,
 ):
     dp = lax.axis_index("dp")
@@ -196,17 +196,20 @@
     pre_hidden += mm(joined[1, own_rows, :], w_proj[1])
     pre_hidden += mm(joined[2, own_rows, :], w_proj[2])
     hidden = silu(pre_hidden).astype(BF)
-    logits = mm_t(w_cls[...], hidden)
+    classes = jnp.concatenate([w_cls[...].astype(F32), jnp.zeros((13, 256), F32)]).astype(BF)
+    for y in range(12):
+        lab[:, y * WIDTH : (y + 1) * WIDTH] = labels[y]
+    logits = mm_t(classes, hidden)
     row = lax.broadcasted_iota(jnp.int32, logits.shape, 0)
     valid = row < 3
     top = jnp.max(jnp.where(valid, logits, -jnp.inf), axis=0, keepdims=True)
     total = jnp.sum(jnp.where(valid, jnp.exp(logits - top), 0.0), axis=0, keepdims=True)
     lse = top + jnp.log(total)
-    onehot = row == labels[...]
+    onehot = row == lab[...]
     loss = jnp.sum(lse - jnp.sum(jnp.where(onehot, logits, 0.0), axis=0, keepdims=True), axis=1, keepdims=True)
     probs = jnp.exp(logits - lse) - jnp.where(onehot, 1.0, 0.0)
     dlogits = jnp.where(valid, probs * loss_scale, 0.0).astype(BF)
-    dhidden = t_mm(dlogits, w_cls[...]) * slope(pre_hidden)
+    dhidden = t_mm(dlogits, classes) * slope(pre_hidden)
     dh[own_rows, :] = dhidden.astype(BF)
     dh_copy = go(remote(dh.at[own_rows], dh.at[own_rows], partner))
 
@@ -251,53 +254,88 @@
         def _(t=t):
             raw_copies[t].start()
 
-    def three(p, phase, buf, landing):
+    low, high = pl.ds(0, 2), pl.ds(2, 2)
+
+    def ring(p, phase, buf, landing):
         axis = ORDERS[p][phase]
         left = [a for a in AXES if a in ORDERS[p][phase:]]
         spot = left.index(axis)
-
-        def chunk(at):
-            return buf.at[(slice(None),) * (1 + spot) + (at,)]
-
-        return [remote(chunk((here[axis] + d) % 4), landing.at[d - 1], peer(axis, d)) for d in (1, 2, 3)], chunk(here[axis])
+        c = here[axis]
+
+        def chunk(at, half=None):
+            index = [slice(None)] * (1 + len(left))
+            index[1 + spot] = (at + 4) % 4
+            if half is not None:
+                index[2 if spot == 0 else 1] = half
+            return buf.at[tuple(index)]
+
+        mine = chunk(c)
+        if phase == 2:
+            return mine, [remote(chunk(c + d), landing.at[d - 1], peer(axis, d)) for d in (1, 2, 3)]
+        up, down = peer(axis, 1), peer(axis, 3)
+
+        def land(slot, half):
+            return landing.at[slot, :, half]
+
+        return mine, [
+            remote(chunk(c + 2, low), land(2, low), up),
+            remote(chunk(c + 2, high), land(2, high), down),
+            remote(chunk(c + 1, high), land(0, high), up),
+            remote(chunk(c - 1, low), land(1, low), down),
+            remote(chunk(c + 1, low), land(0, low), up),
+            remote(chunk(c - 1, high), land(1, high), down),
+        ], [(chunk(c + 1, low), land(2, low)), (chunk(c - 1, high), land(2, high))]
 
     plans = []
     for p in range(4):
         taps = 3 if p < 3 else 1
-        sl = slice(3 * p, 3 * p + 3) if p < 3 else slice(9, 10)
-        first = s1.at[p] if p < 3 else e1
-        lead = pl.ds(sl.start, taps)
-        bufs = (first, s2.at[lead], s3.at[lead])
+        lead = pl.ds(3 * p, taps)
+        bufs = (s1.at[p] if p < 3 else e1, s2.at[lead], s3.at[lead])
         lands = (r1.at[:, lead], r2.at[:, lead], r3.at[:, lead])
-        plan = []
-        for phase in range(3):
-            copies, mine = three(p, phase, bufs[phase], lands[phase])
-            plan.append((copies, mine, lands[phase]))
-        plans.append((plan, bufs, taps, lead))
+        plans.append(([ring(p, phase, bufs[phase], lands[phase]) for phase in range(3)], bufs, lands, taps, 3 * p))
+
+    def firsts(p, phase):
+        copies = plans[p][0][phase][1]
+        return copies if phase == 2 else copies[:4]
 
     def send(p, phase):
-        for copy in plans[p][0][phase][0]:
+        for copy in firsts(p, phase):
             go(copy)
 
+    def each_tap(taps, body):
+        if taps == 1:
+            body(0)
+        else:
+            pl.loop(0, taps)(body)
+
+    def forward(p, phase):
+        (_, copies, sums), taps = plans[p][0][phase], plans[p][3]
+        for n in range(2):
+            copies[n].wait_recv()
+            out, got = sums[n]
+
+            def one(t):
+                out[t] = (out[t].astype(F32) + got[t].astype(F32)).astype(BF)
+
+            each_tap(taps, one)
+            go(copies[4 + n])
+
     def settle(p, phase):
-        plan, bufs, taps, lead = plans[p]
-        copies, mine, landing = plan[phase]
-        for copy in copies:
+        plan, bufs, lands, taps, at = plans[p]
+        mine, copies = plan[phase][:2]
+        for copy in copies if phase == 2 else copies[2:]:
             copy.wait_recv()
 
         def one(t):
             value = mine[t].astype(F32)
-            for d in range(3):
-                value = value + landing[d, t].astype(F32)
+            for n in range(3 if phase == 2 else 2):
+                value = value + lands[phase][n, t].astype(F32)
             if phase < 2:
-                bufs[phase + 1][t] = value.astype(BF)
+                bufs[phase + 1][t] = value.astype(bufs[phase + 1].dtype)
             else:
-                fin[lead.start + t] = value
-
-        if taps == 1:
-            one(0)
-        else:
-            pl.loop(0, taps)(one)
+                fin[at + t] = value
+
+        each_tap(taps, one)
         if phase < 2:
             send(p, phase + 1)
 
@@ -343,12 +381,13 @@
         for p in (1, 2):
             @pl.when((s == p - 1) == toward)
             def _(p=p):
-                for copy in plans[p][0][0][0]:
+                for copy in firsts(p, 0):
                     copy.start()
 
     part(1)
     send(0, 0)
     small_step(0)
+    forward(3, 0)
     part(2 - cross_tap)
     outer_send(False)
     settle(3, 0)
@@ -366,63 +405,74 @@
     part(cross_tap)
     outer_send(True)
     for p in (1, 2):
-        sends.extend(plans[p][0][0][0])
-    small_step(1)
+        sends.extend(firsts(p, 0))
+    forward(0, 0)
+    forward(3, 1)
+    forward(1, 0)
+    forward(2, 0)
     settle(3, 1)
     settle(0, 0)
+    small_step(1)
     settle(3, 2)
 
-    spots = {"x": cx, "z": cz, "y": cy}
-    eout[cx, cz, cy] = fin[9].astype(BF)
-
-    def gather(phase):
-        axis = ORDERS[3][phase]
-        done = ORDERS[3][phase + 1 :]
-        at = tuple(slice(None) if a in done else spots[a] for a in AXES)
-        return [remote(eout.at[at], eout.at[at], peer(axis, d)) for d in (1, 2, 3)]
-
-    gathers = [gather(phase) for phase in range(3)]
-    for copy in gathers[2]:
+    eout[core, cx, cz, cy] = fin[9].astype(BF)
+    everything = slice(None)
+
+    def around(axis, at, half):
+        up, down = peer(axis, 1), peer(axis, 3)
+
+        def view(c, n):
+            index = tuple((c + 4) % 4 if a == axis else v for a, v in zip(AXES, half[n] if n is not None else at))
+            return eout.at[(core,) + index]
+
+        c = here[axis]
+        first = [remote(view(c, None), view(c, None), to) for to in (up, down)]
+        return first, [remote(view(c - 1, 0), view(c - 1, 0), up), remote(view(c + 1, 1), view(c + 1, 1), down)]
+
+    mine = eout.at[core, cx, cz, cy]
+    g_z = [remote(mine, mine, peer("z", d)) for d in (1, 2, 3)]
+    g_y = around("y", (cx, everything, None), ((cx, low, None), (cx, high, None)))
+    g_x = around("x", (None, everything, everything), ((None, low, everything), (None, high, everything)))
+
+    def pass_on(gather):
+        for n in range(2):
+            gather[0][n].wait_recv()
+            go(gather[1][n])
+
+    for copy in g_z:
         go(copy)
+    settle(1, 0)
+    settle(2, 0)
+    forward(0, 1)
+    for copy in g_z:
+        copy.wait_recv()
+    for copy in g_y[0]:
+        go(copy)
+    forward(1, 1)
+    forward(2, 1)
+    pass_on(g_y)
+    settle(0, 1)
     small_step(2)
-    settle(1, 0)
-    for copy in gathers[2]:
+    for copy in g_y[1]:
         copy.wait_recv()
-    for copy in gathers[1]:
+    for copy in g_x[0]:
         go(copy)
-    settle(2, 0)
-    for copy in gathers[1]:
-        copy.wait_recv()
-    for copy in gathers[0]:
-        go(copy)
-    settle(0, 1)
-    small_step(3)
     settle(1, 1)
     settle(2, 1)
-    for copy in gathers[0]:
-        copy.wait_recv()
-    e_swap = go(remote(eout, eoth, partner))
-    settle(0, 2)
-    settle(1, 2)
-    settle(2, 2)
+    pass_on(g_x)
+    small_step(3)
+    for p in range(3):
+        settle(p, 2)
 
     give = pl.ds(pl.multiple_of((1 - core) * 8, 8), 8)
     keep = pl.ds(pl.multiple_of(core * 8, 8), 8)
     swap[0] = fin[0:9, give, :]
     f_swap = go(remote(swap.at[0], swap.at[1], partner))
+    for copy in g_x[1]:
+        copy.wait_recv()
+    e_swap = go(remote(eout.at[core], eout.at[core], partner))
 
     e_swap.wait_recv()
-
-    @pl.when(core == 0)
-    def _():
-        o_proj[...] = eout[0:3].astype(F32).reshape(768, 256)
-        o_one[...] = eoth[...].astype(F32).reshape(1024, 256)
-
-    @pl.when(core == 1)
-    def _():
-        o_proj[...] = eoth[0:3].astype(F32).reshape(768, 256)
-        o_one[...] = eout[...].astype(F32).reshape(1024, 256)
-
     f_swap.wait_recv()
     for p, a in ((0, 1), (1, 0), (2, 2)):
         for b in range(3):
@@ -449,7 +499,15 @@
     assert counter[0] <= COPIES
 
 
-COPIES = 80
+COPIES = 120
+
+
+def widen(scale, shares, small, tiny, o_atr, o_one, o_proj, o_cls, o_loss):
+    o_atr[...] = shares[...]
+    o_proj[...] = small[0, 0:768].astype(F32)
+    o_one[...] = small[1].astype(F32)
+    o_cls[...] = tiny[0:3]
+    o_loss[...] = tiny[3:4, 0:1] * scale
 
 
 def on_device(features, labels, w_one, w_atrous, w_proj, w_class):
@@ -476,27 +534,24 @@
         ((3, 10, 4, 4, 16, 256), BF),
         ((10, 4, 4, 16, 256), BF),
         ((3, 10, 4, 16, 256), BF),
-        ((10, 4, 16, 256), BF),
-        ((3, 10, 16, 256), BF),
+        ((10, 4, 16, 256), F32),
+        ((3, 10, 16, 256), F32),
         ((10, 16, 256), F32),
         ((2, 4, 4, 16, 256), BF),
         ((1, 4, 4, 4, 16, 256), BF),
-        ((4, 4, 4, 16, 256), BF),
-        ((4, 4, 4, 16, 256), BF),
         ((4, 4, 16, 256), F32),
         ((2, 9, 8, 256), F32),
+        ((1, OWN), jnp.int32),
     ]
-    w_cls = jnp.pad(w_class.T, ((0, 13), (0, 0)))
-    out = pl.pallas_call(
+    shares, small, tiny = pl.pallas_call(
         lambda *refs: kernel(1.0 / math.sqrt(total_pix), *refs),
         out_shape=(
             jax.ShapeDtypeStruct((2, 9, 8, 256), F32),
-            jax.ShapeDtypeStruct((1024, 256), F32),
-            jax.ShapeDtypeStruct((768, 256), F32),
+            jax.ShapeDtypeStruct((2, 4, 4, 4, 16, 256), BF),
             jax.ShapeDtypeStruct((16, 256), F32),
         ),
         in_specs=[hbm, vmem, hbm, hbm, vmem, vmem],
-        out_specs=(vmem, vmem, vmem, vmem),
+        out_specs=(vmem, vmem, vmem),
         scratch_shapes=[pltpu.VMEM(shape, kind) for shape, kind in scratch]
         + [
             pltpu.SemaphoreType.DMA((5,)),
@@ -509,19 +564,26 @@
         name="aspp",
     )(
         features.reshape(OWN, 1024),
-        labels.reshape(1, OWN),
+        labels.transpose(1, 0, 2),
         w_one,
         w_atrous,
         w_proj.reshape(3, 256, 256),
-        w_cls,
+        w_class.T,
     )
-    return (
-        out[0].reshape(2, 3, 3, 8, 256),
-        out[1],
-        out[2],
-        out[3][:3].T,
-        out[3][3, 0] / total_pix,
-    )
+    grad_atrous, grad_one, grad_proj, grad_class, loss = pl.pallas_call(
+        lambda *refs: widen(1.0 / total_pix, *refs),
+        out_shape=(
+            jax.ShapeDtypeStruct((2, 9, 8, 256), F32),
+            jax.ShapeDtypeStruct((1024, 256), F32),
+            jax.ShapeDtypeStruct((768, 256), F32),
+            jax.ShapeDtypeStruct((3, 256), F32),
+            jax.ShapeDtypeStruct((1, 1), F32),
+        ),
+        in_specs=[vmem] * 3,
+        out_specs=(vmem,) * 5,
+        name="widen",
+    )(shares, small.reshape(2, 1024, 256), tiny)
+    return (grad_atrous.reshape(2, 3, 3, 8, 256), grad_one, grad_proj, grad_class.T, loss.reshape(()))
 
 
 def solution(mesh):

time: 102 us -> 88.3 us (0.87)
  local copies, waits for them, and re-layouts: 10.3 us -> 0 us
  between operations: 2.43 us -> 0.64 us
    unnamed x3 -> x0, local copies, waits for them, and re-layouts: 5.9 us -> none
    pallas_call x1, Pallas kernels: 87.7 us -> 84.9 us  [on_device(): pl.pallas_call(lambda *refs: kernel(1.0 / math.sqrt(total_pix), *refs), o...]
    pallas_call x0 -> x1, Pallas kernels: none -> 2.57 us  [on_device(): pl.pallas_call(lambda *refs: widen(1.0 / total_pix, *refs), out_shape=(ja...]
    transpose x1 -> x0, local copies, waits for them, and re-layouts: 1.29 us -> none  [on_device(): out[3][:3]]
    pad x1 -> x0, local copies, waits for them, and re-layouts: 1.28 us -> none  [on_device(): w_cls = jnp.pad(w_class.T, ((0, 13), (0, 0)))]
    slice x1 -> x0, local copies, waits for them, and re-layouts: 1.19 us -> none  [on_device(): out[3][3, 0] / total_pix]
where the time goes in v2:
time: 88.3 us; the launch traced here: 88.1 us
  Pallas kernels  87.5 us (99%)
    pallas_call x1, Pallas kernels, on_device(): pl.pallas_call(lambda *refs: kernel(1.0 / math.sqrt(total_pix), *refs), o...  84.9 us
    pallas_call x1, Pallas kernels, on_device(): pl.pallas_call(lambda *refs: widen(1.0 / total_pix, *refs), out_shape=(ja...  2.57 us

profile of v2, /device:TPU:1, one launch (start us, length us, event | category | flops | bytes accessed | tf_op | source)
XLA Modules:
  0.0 88.1 jit_solution(9635048248091825481)
XLA Ops:
  0.6 84.9 %aspp.1 = (f32[2,9,8,256]{3,2,1,0:T(8,128)}, bf16[2,4,4,4,16,256]{5,4,3,2,1,0:T(8,128)(2,1)}, f32[16,256]{1,0:T(8,128)}) custom-call(bf16[672,1024]{1,0:T(8,128)(2,1)} %bitcast.8, s32[12,1,56]{2,1,0:T(1,128)} %bitcast.11, bf16[1024,256]{1,0:T(8,128)(2,1)} %refs_2_.1, bf16[2,3,3,1024,256]{4,3,2,1,0:T(8,128)(2,1)} %refs_3_.1, bf16[3,256,256]{2,1,0:T(8,128)(2,1)} %bitcast.10, ...), custom_call_target="tpu_custom_call" | custom-call | tf_op jit(solution)/shard_map/aspp/pallas_call | solution.py:546
  85.5 2.6 %widen.1 = (f32[2,9,8,256]{3,2,1,0:T(8,128)}, f32[1024,256]{1,0:T(8,128)}, f32[768,256]{1,0:T(8,128)}, f32[3,256]{1,0:T(4,128)}, f32[1,1]{1,0:T(1,128)}) custom-call(f32[2,9,8,256]{3,2,1,0:T(8,128)} %get-tuple-element.13.refs_0_, bf16[2,1024,256]{2,1,0:T(8,128)(2,1)} %bitcast.9, f32[16,256]{1,0:T(8,128)} %get-tuple-element.15.refs_2_), custom_call_target="tpu_custom_call" | custom-call | tf_op jit(solution)/shard_map/widen/pallas_call | solution.py:573

commit v3 on v2

v3 whole, which is shorter than its diff:
```python
import math

import jax
import jax.numpy as jnp
from jax import lax
from jax.experimental import pallas as pl
from jax.experimental.pallas import tpu as pltpu
from jax.sharding import PartitionSpec as P

MESH = pl.DeviceIdType.MESH
BF = jnp.bfloat16
F32 = jnp.float32
WIDTH = 56
BLK = 6 * WIDTH
OWN = 12 * WIDTH
CHIP = 24 * WIDTH
BASE = 3
MIDDLE = ("xzy", "zxy", "zyx")
OUTER = ("xzy", "zxy", "yxz")
SMALL = "xzy"
AXES = "xzy"


def slope(pre):
    gate = jax.nn.sigmoid(pre)
    return gate * (1.0 + pre * (1.0 - gate))


def silu(pre):
    return pre * jax.nn.sigmoid(pre)


def mm(first, second):
    return jnp.dot(first, second, preferred_element_type=F32)


def mm_t(first, second):
    return lax.dot_general(first, second, (((1,), (1,)), ((), ())), preferred_element_type=F32)


def t_mm(first, second):
    return lax.dot_general(first, second, (((0,), (0,)), ((), ())), preferred_element_type=F32)


def kernel(
    loss_scale,
    feat, labels, w_one_h, w_atr_h, w_proj, w_cls,
    o_atr, eout, o_cls,
    xbuf, wbuf, wone, tacc, pre, pre0, cs, cr, joined, dh, ext, db0, raw, hraw,
    s1, r1, s2, r2, s3, r3, fin, pbuf, clbuf, swap, lab,
    lsem, ssem, rsem,
):
    dp = lax.axis_index("dp")
    sp = lax.axis_index("space")
    core, s = sp % 2, sp // 2
    cx, cz, cy = dp // 8, (dp // 2) % 4, (dp % 2) * 2 + s
    here = {"x": cx, "z": cz, "y": cy}

    def place(x, z, y, c):
        return (x * 8 + z * 2 + y // 2, (y % 2) * 2 + c)

    partner = place(cx, cz, cy, 1 - core)
    across = (dp, (1 - s) * 2 + core)

    def peer(axis, d):
        at = dict(here)
        at[axis] = (at[axis] + d) % 4
        return place(at["x"], at["z"], at["y"], core)

    rate = 12 + 6 * core
    k = 2 + core

    counter = [UNITS * 12 + 6]

    def remote(src, dst, to, i=None):
        if i is None:
            i = counter[0]
            counter[0] += 1
        return pltpu.make_async_remote_copy(
            src_ref=src, dst_ref=dst, send_sem=ssem.at[i], recv_sem=rsem.at[i], device_id=to, device_id_type=MESH
        )

    sends = []

    def go(copy):
        copy.start()
        sends.append(copy)
        return copy

    own_rows = pl.ds(pl.multiple_of(core * OWN, 16), OWN)
    other_rows = pl.ds(pl.multiple_of((1 - core) * OWN, 16), OWN)
    x_local = pltpu.make_async_copy(feat, xbuf.at[own_rows], lsem.at[0])
    x_local.start()
    w_local = [pltpu.make_async_copy(w_atr_h.at[core, a], wbuf.at[a], lsem.at[1 + a]) for a in range(3)]
    for a in (1, 0, 2):
        w_local[a].start()
    one_local = pltpu.make_async_copy(w_one_h, wone, lsem.at[4])
    one_local.start()

    barrier = pltpu.get_barrier_semaphore()
    greet = [partner] + [peer(axis, d) for axis in AXES for d in (1, 2, 3)]
    for other in greet:
        pl.semaphore_signal(barrier, inc=1, device_id=other, device_id_type=MESH)

    zero = jnp.zeros((BLK, 256), BF)
    for b in range(3):
        for m in (0, 1, 2, 7, 8, 9):
            ext[b, pl.ds(m * BLK, BLK), :] = zero
    tacc[...] = jnp.zeros_like(tacc)

    column = lax.rem(lax.broadcasted_iota(jnp.int32, (BLK, 256), 0), WIDTH)

    def from_left(value):
        return jnp.where(column >= rate, pltpu.roll(value, rate, 0), 0.0)

    def from_right(value):
        return jnp.where(column < WIDTH - rate, pltpu.roll(value, BLK - rate, 0), 0.0)

    def block(m):
        return pl.ds(pl.multiple_of(m * BLK, 16), BLK)

    def middle(m):
        rows = xbuf[block(m), :]
        for b in range(3):
            tacc[m, b] += mm(rows, wbuf[1, b])

    def outer(m):
        for a in (0, 2):
            to = m - (a - 1) * k

            @pl.when((to >= 0) & (to < 4))
            def _(a=a, to=to):
                rows = xbuf[block(m), :]
                for b in range(3):
                    tacc[to, b] += mm(rows, wbuf[a, b])

    def cross_copy(t):
        return remote(cs.at[t], cr.at[t], across, UNITS * 12 + t)

    cross_tap = s * 2

    def cross(m):
        @pl.when(jnp.where(s == 0, m + k >= 4, m < k))
        def _():
            t = jnp.where(s == 0, m + k - 4, m)
            rows = xbuf[block(m), :]
            parts = [mm(rows, wbuf[cross_tap, b]) for b in range(3)]
            cs[t] = (parts[1] + from_left(parts[0]) + from_right(parts[2])).astype(BF)
            cross_copy(t).start()

    mine, theirs = 2 * core, 2 * (1 - core)
    x_local.wait()
    w_local[1].wait()
    pl.loop(0, 2)(lambda q: middle(mine + q))
    pl.semaphore_wait(barrier, len(greet))
    x_swap = go(remote(feat, xbuf.at[own_rows], partner))
    w_local[0].wait()
    w_local[2].wait()
    pl.loop(0, 2)(lambda q: cross(mine + q))
    pl.loop(0, 2)(lambda q: outer(mine + q))
    x_swap.wait_recv()
    pl.loop(0, 2)(lambda q: cross(theirs + q))

    @pl.loop(0, 2)
    def _(q):
        middle(theirs + q)
        outer(theirs + q)

    @pl.loop(0, 4)
    def _(i):
        pre[block(i), :] = tacc[i, 1] + from_left(tacc[i, 0]) + from_right(tacc[i, 2])

    one_local.wait()

    @pl.when(core == 1)
    def _():
        @pl.loop(0, 4)
        def _(i):
            value = mm(xbuf[block(i), :], wone[...])
            pre0[block(i), :] = value
            joined[0, block(i), :] = silu(value).astype(BF)

    for t in range(3):
        @pl.when(t < k)
        def _(t=t):
            cross_copy(t).wait_recv()
            into = block(jnp.where(s == 0, 4 - k + t, t))
            pre[into, :] += cr[t].astype(F32)

    @pl.loop(0, 4)
    def _(i):
        joined[1 + core, block(i), :] = silu(pre[block(i), :]).astype(BF)

    j_copies = [remote(joined.at[b, other_rows], joined.at[b, other_rows], partner) for b in range(3)]

    @pl.when(core == 0)
    def _():
        j_copies[1].start()

    @pl.when(core == 1)
    def _():
        j_copies[0].start()
        j_copies[2].start()

    @pl.when(core == 0)
    def _():
        j_copies[0].wait_recv()
        j_copies[2].wait_recv()

    @pl.when(core == 1)
    def _():
        j_copies[1].wait_recv()

    pre_hidden = mm(joined[0, own_rows, :], w_proj[0])
    pre_hidden += mm(joined[1, own_rows, :], w_proj[1])
    pre_hidden += mm(joined[2, own_rows, :], w_proj[2])
    hidden = silu(pre_hidden).astype(BF)
    classes = jnp.concatenate([w_cls[...].astype(F32), jnp.zeros((13, 256), F32)]).astype(BF)
    for y in range(12):
        lab[:, y * WIDTH : (y + 1) * WIDTH] = labels[y]
    logits = mm_t(classes, hidden)
    row = lax.broadcasted_iota(jnp.int32, logits.shape, 0)
    valid = row < 3
    top = jnp.max(jnp.where(valid, logits, -jnp.inf), axis=0, keepdims=True)
    total = jnp.sum(jnp.where(valid, jnp.exp(logits - top), 0.0), axis=0, keepdims=True)
    lse = top + jnp.log(total)
    onehot = row == lab[...]
    loss = jnp.sum(lse - jnp.sum(jnp.where(onehot, logits, 0.0), axis=0, keepdims=True), axis=1, keepdims=True)
    probs = jnp.exp(logits - lse) - jnp.where(onehot, 1.0, 0.0)
    dlogits = jnp.where(valid, probs * loss_scale, 0.0).astype(BF)
    dhidden = t_mm(dlogits, classes) * slope(pre_hidden)
    dh[own_rows, :] = dhidden.astype(BF)
    dh_copy = go(remote(dh.at[own_rows], dh.at[own_rows], partner))

    small = mm(dlogits, hidden)
    srow = lax.broadcasted_iota(jnp.int32, small.shape, 0)
    cl_copies = []
    for n, axis in enumerate(AXES):
        cl_copies.append([remote(clbuf.at[n, here[axis]], clbuf.at[n, here[axis]], peer(axis, d)) for d in (1, 2, 3)])
    cl_copies.append([remote(clbuf.at[3, core], clbuf.at[3, core], partner)])
    clbuf[0, here["x"]] = jnp.where(srow == 3, loss, small)
    for copy in cl_copies[0]:
        go(copy)

    def small_step(n):
        for copy in cl_copies[n]:
            copy.wait_recv()
        value = clbuf[n, 0] + clbuf[n, 1]
        if n < 3:
            value = value + clbuf[n, 2] + clbuf[n, 3]
            clbuf[n + 1, core if n == 2 else here[AXES[n + 1]]] = value
            for copy in cl_copies[n + 1]:
                go(copy)
        else:
            o_cls[...] = value

    branch_w = w_proj[1 + core]

    def raw_copy(t):
        return remote(raw.at[block(jnp.where(s == 0, 4 - k + t, t))], hraw.at[t], across, UNITS * 12 + 3 + t)

    def branch_grad(i):
        value = mm_t(dh[block(i), :], branch_w) * slope(pre[block(i), :])
        raw[block(i), :] = value.astype(BF)

        @pl.when(jnp.where(s == 0, i >= 4 - k, i < k))
        def _():
            raw_copy(jnp.where(s == 0, i - (4 - k), i)).start()

        to = block(BASE + i)
        rounded = value.astype(BF).astype(F32)
        ext[0, to, :] = from_right(rounded).astype(BF)
        ext[1, to, :] = rounded.astype(BF)
        ext[2, to, :] = from_left(rounded).astype(BF)

    pl.loop(0, 2)(lambda q: branch_grad(mine + q))
    dh_copy.wait_recv()
    pl.loop(0, 2)(lambda q: branch_grad(theirs + q))

    low, high = pl.ds(0, 2), pl.ds(2, 2)

    def plan(u, order, ring):
        out = []
        for phase, (buf, landing) in enumerate(((s1, r1), (s2, r2), (s3, r3))):
            axis = order[phase]
            left = [a for a in AXES if a in order[phase:]]
            spot = left.index(axis)
            c = here[axis]
            base = u * 12 + (0, 6, 9)[phase]

            def chunk(at, half=None):
                index = [u] + [slice(None)] * len(left)
                index[1 + spot] = (at + 4) % 4
                if half is not None:
                    index[2 if spot == 0 else 1] = half
                return buf.at[tuple(index)]

            def land(slot, half=None):
                return landing.at[u, slot] if half is None else landing.at[u, slot, half]

            if phase or not ring:
                copies = [remote(chunk(c + d), land(d - 1), peer(axis, d), base + d - 1) for d in (2, 1, 3)]
                out.append((chunk(c), [land(n) for n in range(3)], copies, (), (), ()))
                continue
            up, down = peer(axis, 1), peer(axis, 3)
            way = [
                remote(chunk(c + 2, low), land(2, low), up, base),
                remote(chunk(c + 2, high), land(2, high), down, base + 1),
            ]
            copies = [
                remote(chunk(c + 1, high), land(0, high), up, base + 2),
                remote(chunk(c - 1, low), land(1, low), down, base + 3),
            ]
            later = [
                remote(chunk(c + 1, low), land(0, low), up, base + 4),
                remote(chunk(c - 1, high), land(1, high), down, base + 5),
            ]
            sums = [(chunk(c + 1, low), land(2, low)), (chunk(c - 1, high), land(2, high))]
            out.append((chunk(c), [land(0), land(1)], copies, way, later, sums))
        return u, out

    def send(unit, phase):
        _, _, copies, way, _, _ = unit[1][phase]
        for copy in list(way) + copies:
            go(copy)

    def forward(unit):
        _, _, _, way, later, sums = unit[1][0]
        for n in range(2):
            way[n].wait_recv()
            out, got = sums[n]
            out[...] = (out[...].astype(F32) + got[...].astype(F32)).astype(BF)
            go(later[n])

    def settle(unit, phase):
        u, phases = unit
        own, lands, copies, _, later, _ = phases[phase]
        for copy in copies + list(later):
            copy.wait_recv()
        value = own[...].astype(F32)
        for got in lands:
            value = value + got[...].astype(F32)
        if phase < 2:
            into = (s2, s3)[phase]
            into[u] = value.astype(into.dtype)
            send(unit, phase + 1)
        else:
            fin[u] = value

    mids = [plan(b, MIDDLE[b], True) for b in range(3)]
    aways = [plan(3 + 3 * (1 - s) + b, OUTER[b], True) for b in range(3)]
    towards = [plan(3 + 3 * s + b, OUTER[b], True) for b in range(3)]
    smalls = plan(9, SMALL, False)

    def proj_grad(b):
        return t_mm(joined[b], dh[...]).astype(BF).reshape(4, 4, 16, 256)

    p_copies = [remote(pbuf.at[n], s1.at[9, 2 * n], partner) for n in range(2)]

    def tap(u, rows, grad):
        for c in range(4):
            value = t_mm(xbuf[rows, c * 256 : (c + 1) * 256], grad)
            s1[u, c] = value.astype(BF).reshape(4, 4, 16, 256)

    everyone = pl.ds(0, CHIP)

    @pl.when(core == 1)
    def _():
        for n in range(2):
            pbuf[n] = proj_grad(2 * n)
            p_copies[n].start()

        @pl.loop(0, 4)
        def _(i):
            value = mm_t(dh[block(i), :], w_proj[0]) * slope(pre0[block(i), :])
            db0[block(i), :] = value.astype(BF)

        tap(9, everyone, db0[...])

    @pl.when(core == 0)
    def _():
        s1[9, 1] = proj_grad(1)
        s1[9, 3] = jnp.zeros((4, 4, 16, 256), BF)
        for n in range(2):
            p_copies[n].wait_recv()

    send(smalls, 0)

    def rows_from(m, count):
        return pl.ds(pl.multiple_of(m * BLK, 16), count * BLK)

    for b in range(3):
        tap(b, everyone, ext[b, rows_from(BASE, 4), :])
        send(mids[b], 0)
    small_step(0)
    for b in range(3):
        for n in range(2):
            @pl.when(core == n)
            def _(n=n, b=b):
                x_at = jnp.where(s == 0, 2 + n, 0)
                g_at = BASE + jnp.where(s == 0, 0, 2 + n)
                tap(aways[b][0], rows_from(x_at, 2 - n), ext[b, rows_from(g_at, 2 - n), :])
        send(aways[b], 0)

    settle(smalls, 0)
    for b in range(3):
        forward(mids[b])

    for t in range(3):
        @pl.when(t < k)
        def _(t=t):
            raw_copy(t).wait_recv()
            to = block(jnp.where(s == 0, BASE + 4 + t, BASE - k + t))
            value = hraw[t].astype(F32)
            ext[0, to, :] = from_right(value).astype(BF)
            ext[1, to, :] = hraw[t]
            ext[2, to, :] = from_left(value).astype(BF)

    for b in range(3):
        tap(towards[b][0], everyone, ext[b, rows_from(BASE - (cross_tap - 1) * k, 4), :])
        send(towards[b], 0)

    settle(smalls, 1)
    for b in range(2):
        forward(aways[b])
    for b in range(3):
        settle(mids[b], 0)
    small_step(1)
    settle(smalls, 2)

    eout[core, cx, cz, cy] = fin[9].astype(BF)
    everything = slice(None)

    def gather(axis, at):
        view = eout.at[(core,) + at]
        return [remote(view, view, peer(axis, d)) for d in (2, 1, 3)]

    gathers = [gather("z", (cx, cz, cy)), gather("y", (cx, everything, cy)), gather("x", (cx, everything, everything))]

    def gather_next(n):
        for copy in gathers[n - 1] if n else ():
            copy.wait_recv()
        for copy in gathers[n] if n < 3 else ():
            go(copy)

    gather_next(0)
    for b in range(2):
        settle(aways[b], 0)
    for b in range(2):
        forward(towards[b])
    for b in range(3):
        settle(mids[b], 1)
    gather_next(1)
    small_step(2)
    forward(aways[2])
    forward(towards[2])
    for b in range(2):
        settle(aways[b], 1)
    for b in range(2):
        settle(towards[b], 0)
    gather_next(2)
    for b in range(3):
        settle(mids[b], 2)
    settle(aways[2], 0)
    settle(towards[2], 0)
    for b in range(2):
        settle(towards[b], 1)
    for b in range(2):
        settle(aways[b], 2)
    gather_next(3)
    e_swap = go(remote(eout.at[core], eout.at[core], partner))
    small_step(3)
    settle(aways[2], 1)
    settle(towards[2], 1)
    for b in range(2):
        settle(towards[b], 2)
    settle(aways[2], 2)
    settle(towards[2], 2)

    give = pl.ds(pl.multiple_of((1 - core) * 8, 8), 8)
    keep = pl.ds(pl.multiple_of(core * 8, 8), 8)
    swap[0] = fin[0:9, give, :]
    f_swap = go(remote(swap.at[0], swap.at[1], partner))

    e_swap.wait_recv()
    f_swap.wait_recv()
    for u in range(9):
        at = u + 3 if u < 3 else u - 3 if u < 6 else u
        o_atr[core, at] = fin[u, keep, :]
        o_atr[1 - core, at] = swap[1, u]

    for t in range(3):
        @pl.when(t < k)
        def _(t=t):
            cross_copy(t).wait_send()
            raw_copy(t).wait_send()

    @pl.when(core == 0)
    def _():
        j_copies[1].wait_send()

    @pl.when(core == 1)
    def _():
        for copy in (j_copies[0], j_copies[2], p_copies[0], p_copies[1]):
            copy.wait_send()

    for copy in sends:
        copy.wait_send()
    assert counter[0] <= COPIES


COPIES = 180
UNITS = 10


def widen(scale, shares, small, tiny, o_atr, o_one, o_proj, o_cls, o_loss):
    o_atr[...] = shares[...]
    o_proj[...] = small[0, 0:768].astype(F32)
    o_one[...] = small[1].astype(F32)
    o_cls[...] = tiny[0:3]
    o_loss[...] = tiny[3:4, 0:1] * scale


def on_device(features, labels, w_one, w_atrous, w_proj, w_class):
    total_pix = lax.axis_size("dp") * lax.axis_size("space") * OWN
    vmem = pl.BlockSpec(memory_space=pltpu.VMEM)
    hbm = pl.BlockSpec(memory_space=pl.ANY)
    scratch = [
        ((CHIP, 1024), BF),
        ((3, 3, 1024, 256), BF),
        ((1024, 256), BF),
        ((4, 3, BLK, 256), F32),
        ((CHIP, 256), F32),
        ((CHIP, 256), F32),
        ((3, BLK, 256), BF),
        ((3, BLK, 256), BF),
        ((3, CHIP, 256), BF),
        ((CHIP, 256), BF),
        ((3, 10 * BLK, 256), BF),
        ((CHIP, 256), BF),
        ((CHIP, 256), BF),
        ((3, BLK, 256), BF),
        ((UNITS, 4, 4, 4, 16, 256), BF),
        ((UNITS, 3, 4, 4, 16, 256), BF),
        ((UNITS, 4, 4, 16, 256), BF),
        ((UNITS, 3, 4, 16, 256), BF),
        ((UNITS, 4, 16, 256), F32),
        ((UNITS, 3, 16, 256), F32),
        ((UNITS, 16, 256), F32),
        ((2, 4, 4, 16, 256), BF),
        ((4, 4, 16, 256), F32),
        ((2, 9, 8, 256), F32),
        ((1, OWN), jnp.int32),
    ]
    shares, small, tiny = pl.pallas_call(
        lambda *refs: kernel(1.0 / math.sqrt(total_pix), *refs),
        out_shape=(
            jax.ShapeDtypeStruct((2, 9, 8, 256), F32),
            jax.ShapeDtypeStruct((2, 4, 4, 4, 16, 256), BF),
            jax.ShapeDtypeStruct((16, 256), F32),
        ),
        in_specs=[hbm, vmem, hbm, hbm, vmem, vmem],
        out_specs=(vmem, vmem, vmem),
        scratch_shapes=[pltpu.VMEM(shape, kind) for shape, kind in scratch]
        + [
            pltpu.SemaphoreType.DMA((5,)),
            pltpu.SemaphoreType.DMA((COPIES,)),
            pltpu.SemaphoreType.DMA((COPIES,)),
        ],
        compiler_params=pltpu.CompilerParams(
            collective_id=0, has_side_effects=True, vmem_limit_bytes=60 * 1024 * 1024
        ),
        name="aspp",
    )(
        features.reshape(OWN, 1024),
        labels.transpose(1, 0, 2),
        w_one,
        w_atrous,
        w_proj.reshape(3, 256, 256),
        w_class.T,
    )
    grad_atrous, grad_one, grad_proj, grad_class, loss = pl.pallas_call(
        lambda *refs: widen(1.0 / total_pix, *refs),
        out_shape=(
            jax.ShapeDtypeStruct((2, 9, 8, 256), F32),
            jax.ShapeDtypeStruct((1024, 256), F32),
            jax.ShapeDtypeStruct((768, 256), F32),
            jax.ShapeDtypeStruct((3, 256), F32),
            jax.ShapeDtypeStruct((1, 1), F32),
        ),
        in_specs=[vmem] * 3,
        out_specs=(vmem,) * 5,
        name="widen",
    )(shares, small.reshape(2, 1024, 256), tiny)
    return (grad_atrous.reshape(2, 3, 3, 8, 256), grad_one, grad_proj, grad_class.T, loss.reshape(()))


def solution(mesh):
    return jax.shard_map(
        on_device,
        mesh=mesh,
        in_specs=(P("dp", "space", None, None), P("dp", "space", None), P(), P(), P(), P()),
        out_specs=(P(None, None, None, ("dp", "space"), None), P(), P(), P(), P()),
        check_vma=False,
    )
```

time: 88.3 us -> 82.1 us (0.930)
  Pallas kernels: 87.5 us -> 81.3 us
    pallas_call x1, Pallas kernels: 84.9 us -> 78.8 us  [on_device(): pl.pallas_call(lambda *refs: kernel(1.0 / math.sqrt(total_pix), *refs), o...]
where the time goes in v3:
time: 82.1 us; the launch traced here: 82 us
  Pallas kernels  81.3 us (99%)
    pallas_call x1, Pallas kernels, on_device(): pl.pallas_call(lambda *refs: kernel(1.0 / math.sqrt(total_pix), *refs), o...  78.8 us
    pallas_call x1, Pallas kernels, on_device(): pl.pallas_call(lambda *refs: widen(1.0 / total_pix, *refs), out_shape=(ja...  2.57 us

profile of v3, /device:TPU:1, one launch (start us, length us, event | category | flops | bytes accessed | tf_op | source)
XLA Modules:
  0.0 82.0 jit_solution(5116693858852173008)
XLA Ops:
  0.6 78.8 %aspp.1 = (f32[2,9,8,256]{3,2,1,0:T(8,128)}, bf16[2,4,4,4,16,256]{5,4,3,2,1,0:T(8,128)(2,1)}, f32[16,256]{1,0:T(8,128)}) custom-call(bf16[672,1024]{1,0:T(8,128)(2,1)} %bitcast.8, s32[12,1,56]{2,1,0:T(1,128)} %bitcast.11, bf16[1024,256]{1,0:T(8,128)(2,1)} %refs_2_.1, bf16[2,3,3,1024,256]{4,3,2,1,0:T(8,128)(2,1)} %refs_3_.1, bf16[3,256,256]{2,1,0:T(8,128)(2,1)} %bitcast.10, ...), custom_call_target="tpu_custom_call" | custom-call | tf_op jit(solution)/shard_map/aspp/pallas_call | solution.py:555
  79.4 2.6 %widen.1 = (f32[2,9,8,256]{3,2,1,0:T(8,128)}, f32[1024,256]{1,0:T(8,128)}, f32[768,256]{1,0:T(8,128)}, f32[3,256]{1,0:T(4,128)}, f32[1,1]{1,0:T(1,128)}) custom-call(f32[2,9,8,256]{3,2,1,0:T(8,128)} %get-tuple-element.13.refs_0_, bf16[2,1024,256]{2,1,0:T(8,128)(2,1)} %bitcast.9, f32[16,256]{1,0:T(8,128)} %get-tuple-element.15.refs_2_), custom_call_target="tpu_custom_call" | custom-call | tf_op jit(solution)/shard_map/widen/pallas_call | solution.py:582

commit v4 on v3

--- a/solution.py
+++ b/solution.py
@@ -14,10 +14,10 @@
 BLK = 6 * WIDTH
 OWN = 12 * WIDTH
 CHIP = 24 * WIDTH
-BASE = 3
-MIDDLE = ("xzy", "zxy", "zyx")
-OUTER = ("xzy", "zxy", "yxz")
-SMALL = "xzy"
+BASE = 1
+XB = 2
+ORDER = ("xzy", "zyx", "yxz")
+SMALL = "yzx"
 AXES = "xzy"
 
 
@@ -61,6 +61,7 @@
 
     partner = place(cx, cz, cy, 1 - core)
     across = (dp, (1 - s) * 2 + core)
+    beyond = (dp, (1 - s) * 2 + 1 - core)
 
     def peer(axis, d):
         at = dict(here)
@@ -70,7 +71,7 @@
     rate = 12 + 6 * core
     k = 2 + core
 
-    counter = [UNITS * 12 + 6]
+    counter = [UNITS * 12 + 7]
 
     def remote(src, dst, to, i=None):
         if i is None:
@@ -89,7 +90,8 @@
 
     own_rows = pl.ds(pl.multiple_of(core * OWN, 16), OWN)
     other_rows = pl.ds(pl.multiple_of((1 - core) * OWN, 16), OWN)
-    x_local = pltpu.make_async_copy(feat, xbuf.at[own_rows], lsem.at[0])
+    x_own = pl.ds(pl.multiple_of(XB * BLK + core * OWN, 16), OWN)
+    x_local = pltpu.make_async_copy(feat, xbuf.at[x_own], lsem.at[0])
     x_local.start()
     w_local = [pltpu.make_async_copy(w_atr_h.at[core, a], wbuf.at[a], lsem.at[1 + a]) for a in range(3)]
     for a in (1, 0, 2):
@@ -98,14 +100,10 @@
     one_local.start()
 
     barrier = pltpu.get_barrier_semaphore()
-    greet = [partner] + [peer(axis, d) for axis in AXES for d in (1, 2, 3)]
+    greet = [partner, beyond] + [peer(axis, d) for axis in AXES for d in (1, 2, 3)]
     for other in greet:
         pl.semaphore_signal(barrier, inc=1, device_id=other, device_id_type=MESH)
 
-    zero = jnp.zeros((BLK, 256), BF)
-    for b in range(3):
-        for m in (0, 1, 2, 7, 8, 9):
-            ext[b, pl.ds(m * BLK, BLK), :] = zero
     tacc[...] = jnp.zeros_like(tacc)
 
     column = lax.rem(lax.broadcasted_iota(jnp.int32, (BLK, 256), 0), WIDTH)
@@ -120,7 +118,7 @@
         return pl.ds(pl.multiple_of(m * BLK, 16), BLK)
 
     def middle(m):
-        rows = xbuf[block(m), :]
+        rows = xbuf[block(XB + m), :]
         for b in range(3):
             tacc[m, b] += mm(rows, wbuf[1, b])
 
@@ -130,7 +128,7 @@
 
             @pl.when((to >= 0) & (to < 4))
             def _(a=a, to=to):
-                rows = xbuf[block(m), :]
+                rows = xbuf[block(XB + m), :]
                 for b in range(3):
                     tacc[to, b] += mm(rows, wbuf[a, b])
 
@@ -143,7 +141,7 @@
         @pl.when(jnp.where(s == 0, m + k >= 4, m < k))
         def _():
             t = jnp.where(s == 0, m + k - 4, m)
-            rows = xbuf[block(m), :]
+            rows = xbuf[block(XB + m), :]
             parts = [mm(rows, wbuf[cross_tap, b]) for b in range(3)]
             cs[t] = (parts[1] + from_left(parts[0]) + from_right(parts[2])).astype(BF)
             cross_copy(t).start()
@@ -153,7 +151,7 @@
     w_local[1].wait()
     pl.loop(0, 2)(lambda q: middle(mine + q))
     pl.semaphore_wait(barrier, len(greet))
-    x_swap = go(remote(feat, xbuf.at[own_rows], partner))
+    x_swap = go(remote(feat, xbuf.at[x_own], partner))
     w_local[0].wait()
     w_local[2].wait()
     pl.loop(0, 2)(lambda q: cross(mine + q))
@@ -166,6 +164,15 @@
         middle(theirs + q)
         outer(theirs + q)
 
+    def halo(j):
+        to = block(jnp.where(s == 0, j, XB + 4 + j))
+        return remote(feat.at[j * BLK : (j + 1) * BLK], xbuf.at[to], (dp, (1 - s) * 2 + j), UNITS * 12 + 4 + j)
+
+    @pl.when(core == 1 - s)
+    def _():
+        for j in range(2):
+            halo(j).start()
+
     @pl.loop(0, 4)
     def _(i):
         pre[block(i), :] = tacc[i, 1] + from_left(tacc[i, 0]) + from_right(tacc[i, 2])
@@ -176,7 +183,7 @@
     def _():
         @pl.loop(0, 4)
         def _(i):
-            value = mm(xbuf[block(i), :], wone[...])
+            value = mm(xbuf[block(XB + i), :], wone[...])
             pre0[block(i), :] = value
             joined[0, block(i), :] = silu(value).astype(BF)
 
@@ -256,16 +263,15 @@
 
     branch_w = w_proj[1 + core]
 
-    def raw_copy(t):
-        return remote(raw.at[block(jnp.where(s == 0, 4 - k + t, t))], hraw.at[t], across, UNITS * 12 + 3 + t)
+    raw_copy = remote(raw.at[block(jnp.where(s == 0, 3, 0))], hraw, across, UNITS * 12 + 3)
 
     def branch_grad(i):
         value = mm_t(dh[block(i), :], branch_w) * slope(pre[block(i), :])
         raw[block(i), :] = value.astype(BF)
 
-        @pl.when(jnp.where(s == 0, i >= 4 - k, i < k))
+        @pl.when((core == 1) & (i == jnp.where(s == 0, 3, 0)))
         def _():
-            raw_copy(jnp.where(s == 0, i - (4 - k), i)).start()
+            raw_copy.start()
 
         to = block(BASE + i)
         rounded = value.astype(BF).astype(F32)
@@ -347,9 +353,10 @@
         else:
             fin[u] = value
 
-    mids = [plan(b, MIDDLE[b], True) for b in range(3)]
-    aways = [plan(3 + 3 * (1 - s) + b, OUTER[b], True) for b in range(3)]
-    towards = [plan(3 + 3 * s + b, OUTER[b], True) for b in range(3)]
+    mids = [plan(b, ORDER[b], True) for b in range(3)]
+    outers = [plan(3 + 3 * g + b, ORDER[b], True) for b in range(3) for g in range(2)]
+    nears = [plan(3 + 3 * s + b, ORDER[b], True) for b in range(3)]
+    fars = [plan(3 + 3 * (1 - s) + b, ORDER[b], True) for b in range(3)]
     smalls = plan(9, SMALL, False)
 
     def proj_grad(b):
@@ -362,7 +369,7 @@
             value = t_mm(xbuf[rows, c * 256 : (c + 1) * 256], grad)
             s1[u, c] = value.astype(BF).reshape(4, 4, 16, 256)
 
-    everyone = pl.ds(0, CHIP)
+    everyone = pl.ds(XB * BLK, CHIP)
 
     @pl.when(core == 1)
     def _():
@@ -393,38 +400,46 @@
         tap(b, everyone, ext[b, rows_from(BASE, 4), :])
         send(mids[b], 0)
     small_step(0)
+
+    @pl.when(core == 1)
+    def _():
+        raw_copy.wait_recv()
+        to = block(jnp.where(s == 0, BASE + 4, BASE - 1))
+        value = hraw[...].astype(F32)
+        ext[0, to, :] = from_right(value).astype(BF)
+        ext[1, to, :] = hraw[...]
+        ext[2, to, :] = from_left(value).astype(BF)
+
+    passed_rows = block(jnp.where(s == 0, XB + 4, 0) + core)
+    remote(feat.at[0:BLK], xbuf.at[passed_rows], across, UNITS * 12 + 4 + core).wait_recv()
+    passed = go(remote(xbuf.at[passed_rows], xbuf.at[passed_rows], partner, UNITS * 12 + 6))
+
+    for b in range(3):
+        x_at = XB + jnp.where(s == 0, 0, 2)
+        g_at = BASE + jnp.where(s == 0, k, 2 - k)
+        tap(nears[b][0], rows_from(x_at, 2), ext[b, rows_from(g_at, 2), :])
+        send(nears[b], 0)
+
+    passed.wait_recv()
     for b in range(3):
         for n in range(2):
             @pl.when(core == n)
             def _(n=n, b=b):
-                x_at = jnp.where(s == 0, 2 + n, 0)
-                g_at = BASE + jnp.where(s == 0, 0, 2 + n)
-                tap(aways[b][0], rows_from(x_at, 2 - n), ext[b, rows_from(g_at, 2 - n), :])
-        send(aways[b], 0)
-
+                x_at = jnp.where(s == 0, XB + 2 + n, 0)
+                g_at = BASE + jnp.where(s == 0, 0, n)
+                tap(fars[b][0], rows_from(x_at, 4 - n), ext[b, rows_from(g_at, 4 - n), :])
+        send(fars[b], 0)
+
+    for unit in mids:
+        forward(unit)
     settle(smalls, 0)
-    for b in range(3):
-        forward(mids[b])
-
-    for t in range(3):
-        @pl.when(t < k)
-        def _(t=t):
-            raw_copy(t).wait_recv()
-            to = block(jnp.where(s == 0, BASE + 4 + t, BASE - k + t))
-            value = hraw[t].astype(F32)
-            ext[0, to, :] = from_right(value).astype(BF)
-            ext[1, to, :] = hraw[t]
-            ext[2, to, :] = from_left(value).astype(BF)
-
-    for b in range(3):
-        tap(towards[b][0], everyone, ext[b, rows_from(BASE - (cross_tap - 1) * k, 4), :])
-        send(towards[b], 0)
-
+    for unit in outers:
+        forward(unit)
+    for unit in mids:
+        settle(unit, 0)
     settle(smalls, 1)
-    for b in range(2):
-        forward(aways[b])
-    for b in range(3):
-        settle(mids[b], 0)
+    for unit in outers:
+        settle(unit, 0)
     small_step(1)
     settle(smalls, 2)
 
@@ -444,43 +459,25 @@
             go(copy)
 
     gather_next(0)
-    for b in range(2):
-        settle(aways[b], 0)
-    for b in range(2):
-        forward(towards[b])
-    for b in range(3):
-        settle(mids[b], 1)
+    for unit in mids:
+        settle(unit, 1)
     gather_next(1)
+    for unit in outers:
+        settle(unit, 1)
+    gather_next(2)
     small_step(2)
-    forward(aways[2])
-    forward(towards[2])
-    for b in range(2):
-        settle(aways[b], 1)
-    for b in range(2):
-        settle(towards[b], 0)
-    gather_next(2)
-    for b in range(3):
-        settle(mids[b], 2)
-    settle(aways[2], 0)
-    settle(towards[2], 0)
-    for b in range(2):
-        settle(towards[b], 1)
-    for b in range(2):
-        settle(aways[b], 2)
-    gather_next(3)
-    e_swap = go(remote(eout.at[core], eout.at[core], partner))
-    small_step(3)
-    settle(aways[2], 1)
-    settle(towards[2], 1)
-    for b in range(2):
-        settle(towards[b], 2)
-    settle(aways[2], 2)
-    settle(towards[2], 2)
+    for unit in mids:
+        settle(unit, 2)
+    for unit in outers:
+        settle(unit, 2)
 
     give = pl.ds(pl.multiple_of((1 - core) * 8, 8), 8)
     keep = pl.ds(pl.multiple_of(core * 8, 8), 8)
     swap[0] = fin[0:9, give, :]
     f_swap = go(remote(swap.at[0], swap.at[1], partner))
+    small_step(3)
+    gather_next(3)
+    e_swap = go(remote(eout.at[core], eout.at[core], partner))
 
     e_swap.wait_recv()
     f_swap.wait_recv()
@@ -493,7 +490,15 @@
         @pl.when(t < k)
         def _(t=t):
             cross_copy(t).wait_send()
-            raw_copy(t).wait_send()
+
+    @pl.when(core == 1 - s)
+    def _():
+        for j in range(2):
+            halo(j).wait_send()
+
+    @pl.when(core == 1)
+    def _():
+        raw_copy.wait_send()
 
     @pl.when(core == 0)
     def _():
@@ -526,7 +531,7 @@
     vmem = pl.BlockSpec(memory_space=pltpu.VMEM)
     hbm = pl.BlockSpec(memory_space=pl.ANY)
     scratch = [
-        ((CHIP, 1024), BF),
+        ((8 * BLK, 1024), BF),
         ((3, 3, 1024, 256), BF),
         ((1024, 256), BF),
         ((4, 3, BLK, 256), F32),
@@ -536,10 +541,10 @@
         ((3, BLK, 256), BF),
         ((3, CHIP, 256), BF),
         ((CHIP, 256), BF),
-        ((3, 10 * BLK, 256), BF),
+        ((3, 6 * BLK, 256), BF),
         ((CHIP, 256), BF),
         ((CHIP, 256), BF),
-        ((3, BLK, 256), BF),
+        ((BLK, 256), BF),
         ((UNITS, 4, 4, 4, 16, 256), BF),
         ((UNITS, 3, 4, 4, 16, 256), BF),
         ((UNITS, 4, 4, 16, 256), BF),

time: 82.1 us -> 82.7 us (level)
  no operation moved by 1% of the time
where the time goes in v4:
time: 82.7 us; the launch traced here: 82.5 us
  Pallas kernels  81.9 us (99%)
    pallas_call x1, Pallas kernels, on_device(): pl.pallas_call(lambda *refs: kernel(1.0 / math.sqrt(total_pix), *refs), o...  79.3 us
    pallas_call x1, Pallas kernels, on_device(): pl.pallas_call(lambda *refs: widen(1.0 / total_pix, *refs), out_shape=(ja...  2.57 us

profile of v4, /device:TPU:1, one launch (start us, length us, event | category | flops | bytes accessed | tf_op | source)
XLA Modules:
  0.0 82.5 jit_solution(14417627419142542033)
XLA Ops:
  0.6 79.3 %aspp.1 = (f32[2,9,8,256]{3,2,1,0:T(8,128)}, bf16[2,4,4,4,16,256]{5,4,3,2,1,0:T(8,128)(2,1)}, f32[16,256]{1,0:T(8,128)}) custom-call(bf16[672,1024]{1,0:T(8,128)(2,1)} %bitcast.8, s32[12,1,56]{2,1,0:T(1,128)} %bitcast.11, bf16[1024,256]{1,0:T(8,128)(2,1)} %refs_2_.1, bf16[2,3,3,1024,256]{4,3,2,1,0:T(8,128)(2,1)} %refs_3_.1, bf16[3,256,256]{2,1,0:T(8,128)(2,1)} %bitcast.10, ...), custom_call_target="tpu_custom_call" | custom-call | tf_op jit(solution)/shard_map/aspp/pallas_call | solution.py:560
  80.0 2.6 %widen.1 = (f32[2,9,8,256]{3,2,1,0:T(8,128)}, f32[1024,256]{1,0:T(8,128)}, f32[768,256]{1,0:T(8,128)}, f32[3,256]{1,0:T(4,128)}, f32[1,1]{1,0:T(1,128)}) custom-call(f32[2,9,8,256]{3,2,1,0:T(8,128)} %get-tuple-element.13.refs_0_, bf16[2,1024,256]{2,1,0:T(8,128)(2,1)} %bitcast.9, f32[16,256]{1,0:T(8,128)} %get-tuple-element.15.refs_2_), custom_call_target="tpu_custom_call" | custom-call | tf_op jit(solution)/shard_map/widen/pallas_call | solution.py:587

commit v5 on v4

--- a/solution.py
+++ b/solution.py
@@ -46,7 +46,7 @@
     loss_scale,
     feat, labels, w_one_h, w_atr_h, w_proj, w_cls,
     o_atr, eout, o_cls,
-    xbuf, wbuf, wone, tacc, pre, pre0, cs, cr, joined, dh, ext, db0, raw, hraw,
+    xbuf, wbuf, wtow, wone, tacc, pre, pre0, cs, cr, joined, dh, ext, db0, raw, hraw,
     s1, r1, s2, r2, s3, r3, fin, pbuf, clbuf, swap, lab,
     lsem, ssem, rsem,
 ):
@@ -71,14 +71,14 @@
     rate = 12 + 6 * core
     k = 2 + core
 
-    counter = [UNITS * 12 + 7]
-
-    def remote(src, dst, to, i=None):
+    counter = [UNITS * 12 + 13]
+
+    def remote(src, dst, to, i=None, sent=None):
         if i is None:
             i = counter[0]
             counter[0] += 1
         return pltpu.make_async_remote_copy(
-            src_ref=src, dst_ref=dst, send_sem=ssem.at[i], recv_sem=rsem.at[i], device_id=to, device_id_type=MESH
+            src_ref=src, dst_ref=dst, send_sem=ssem.at[i if sent is None else sent], recv_sem=rsem.at[i], device_id=to, device_id_type=MESH
         )
 
     sends = []
@@ -94,8 +94,10 @@
     x_local = pltpu.make_async_copy(feat, xbuf.at[x_own], lsem.at[0])
     x_local.start()
     w_local = [pltpu.make_async_copy(w_atr_h.at[core, a], wbuf.at[a], lsem.at[1 + a]) for a in range(3)]
-    for a in (1, 0, 2):
-        w_local[a].start()
+    cross_tap = s * 2
+    tow_local = [pltpu.make_async_copy(w_atr_h.at[g, cross_tap], wtow.at[g], lsem.at[5 + g]) for g in range(2)]
+    for copy in (tow_local[1], tow_local[0], w_local[1], w_local[0], w_local[2]):
+        copy.start()
     one_local = pltpu.make_async_copy(w_one_h, wone, lsem.at[4])
     one_local.start()
 
@@ -108,10 +110,10 @@
 
     column = lax.rem(lax.broadcasted_iota(jnp.int32, (BLK, 256), 0), WIDTH)
 
-    def from_left(value):
+    def from_left(value, rate=rate):
         return jnp.where(column >= rate, pltpu.roll(value, rate, 0), 0.0)
 
-    def from_right(value):
+    def from_right(value, rate=rate):
         return jnp.where(column < WIDTH - rate, pltpu.roll(value, BLK - rate, 0), 0.0)
 
     def block(m):
@@ -132,32 +134,39 @@
                 for b in range(3):
                     tacc[to, b] += mm(rows, wbuf[a, b])
 
-    def cross_copy(t):
-        return remote(cs.at[t], cr.at[t], across, UNITS * 12 + t)
-
-    cross_tap = s * 2
-
-    def cross(m):
-        @pl.when(jnp.where(s == 0, m + k >= 4, m < k))
-        def _():
-            t = jnp.where(s == 0, m + k - 4, m)
-            rows = xbuf[block(XB + m), :]
-            parts = [mm(rows, wbuf[cross_tap, b]) for b in range(3)]
-            cs[t] = (parts[1] + from_left(parts[0]) + from_right(parts[2])).astype(BF)
-            cross_copy(t).start()
+    def cross_copy(t, g=None):
+        if g is None:
+            return remote(cs.at[0, t], cr.at[t], across, UNITS * 12 + t)
+        to = (dp, (1 - s) * 2 + g)
+        return remote(cs.at[g, t], cr.at[t], to, UNITS * 12 + t, UNITS * 12 + 7 + 3 * g + t)
+
+    def crossing(body):
+        for g, t in ((1, 0), (1, 1), (1, 2), (0, 0), (0, 1)):
+            m = jnp.where(s == 0, 2 - g + t, t)
+
+            @pl.when(m // 2 == core)
+            def _(g=g, t=t, m=m):
+                body(g, t, m)
+
+    def cross(g, t, m):
+        rows = xbuf[block(XB + m), :]
+        parts = [mm(rows, wtow[g, b]) for b in range(3)]
+        shifted = from_left(parts[0], 12 + 6 * g) + from_right(parts[2], 12 + 6 * g)
+        cs[g, t] = (parts[1] + shifted).astype(BF)
 
     mine, theirs = 2 * core, 2 * (1 - core)
     x_local.wait()
-    w_local[1].wait()
+    for copy in tow_local:
+        copy.wait()
+    crossing(cross)
+    pl.semaphore_wait(barrier, len(greet))
+    crossing(lambda g, t, m: cross_copy(t, g).start())
+    x_swap = go(remote(feat, xbuf.at[x_own], partner))
+    for copy in (w_local[1], w_local[0], w_local[2]):
+        copy.wait()
     pl.loop(0, 2)(lambda q: middle(mine + q))
-    pl.semaphore_wait(barrier, len(greet))
-    x_swap = go(remote(feat, xbuf.at[x_own], partner))
-    w_local[0].wait()
-    w_local[2].wait()
-    pl.loop(0, 2)(lambda q: cross(mine + q))
     pl.loop(0, 2)(lambda q: outer(mine + q))
     x_swap.wait_recv()
-    pl.loop(0, 2)(lambda q: cross(theirs + q))
 
     @pl.loop(0, 2)
     def _(q):
@@ -420,6 +429,9 @@
         tap(nears[b][0], rows_from(x_at, 2), ext[b, rows_from(g_at, 2), :])
         send(nears[b], 0)
 
+    for unit in mids:
+        forward(unit)
+    settle(smalls, 0)
     passed.wait_recv()
     for b in range(3):
         for n in range(2):
@@ -430,17 +442,9 @@
                 tap(fars[b][0], rows_from(x_at, 4 - n), ext[b, rows_from(g_at, 4 - n), :])
         send(fars[b], 0)
 
-    for unit in mids:
-        forward(unit)
-    settle(smalls, 0)
+    settle(smalls, 1)
     for unit in outers:
         forward(unit)
-    for unit in mids:
-        settle(unit, 0)
-    settle(smalls, 1)
-    for unit in outers:
-        settle(unit, 0)
-    small_step(1)
     settle(smalls, 2)
 
     eout[core, cx, cz, cy] = fin[9].astype(BF)
@@ -460,12 +464,19 @@
 
     gather_next(0)
     for unit in mids:
-        settle(unit, 1)
+        settle(unit, 0)
+    small_step(1)
     gather_next(1)
     for unit in outers:
+        settle(unit, 0)
+    gather_next(2)
+    for unit in mids:
         settle(unit, 1)
-    gather_next(2)
     small_step(2)
+    for unit in outers:
+        settle(unit, 1)
+    gather_next(3)
+    e_swap = go(remote(eout.at[core], eout.at[core], partner))
     for unit in mids:
         settle(unit, 2)
     for unit in outers:
@@ -476,8 +487,6 @@
     swap[0] = fin[0:9, give, :]
     f_swap = go(remote(swap.at[0], swap.at[1], partner))
     small_step(3)
-    gather_next(3)
-    e_swap = go(remote(eout.at[core], eout.at[core], partner))
 
     e_swap.wait_recv()
     f_swap.wait_recv()
@@ -486,10 +495,7 @@
         o_atr[core, at] = fin[u, keep, :]
         o_atr[1 - core, at] = swap[1, u]
 
-    for t in range(3):
-        @pl.when(t < k)
-        def _(t=t):
-            cross_copy(t).wait_send()
+    crossing(lambda g, t, m: cross_copy(t, g).wait_send())
 
     @pl.when(core == 1 - s)
     def _():
@@ -533,11 +539,12 @@
     scratch = [
         ((8 * BLK, 1024), BF),
         ((3, 3, 1024, 256), BF),
+        ((2, 3, 1024, 256), BF),
         ((1024, 256), BF),
         ((4, 3, BLK, 256), F32),
         ((CHIP, 256), F32),
         ((CHIP, 256), F32),
-        ((3, BLK, 256), BF),
+        ((2, 3, BLK, 256), BF),
         ((3, BLK, 256), BF),
         ((3, CHIP, 256), BF),
         ((CHIP, 256), BF),
@@ -568,7 +575,7 @@
         out_specs=(vmem, vmem, vmem),
         scratch_shapes=[pltpu.VMEM(shape, kind) for shape, kind in scratch]
         + [
-            pltpu.SemaphoreType.DMA((5,)),
+            pltpu.SemaphoreType.DMA((7,)),
             pltpu.SemaphoreType.DMA((COPIES,)),
             pltpu.SemaphoreType.DMA((COPIES,)),
         ],

time: 82.7 us -> 82.9 us (level)
  no operation moved by 1% of the time
where the time goes in v5:
time: 82.9 us; the launch traced here: 82.7 us
  Pallas kernels  82.1 us (99%)
    pallas_call x1, Pallas kernels, on_device(): pl.pallas_call(lambda *refs: kernel(1.0 / math.sqrt(total_pix), *refs), o...  79.5 us
    pallas_call x1, Pallas kernels, on_device(): pl.pallas_call(lambda *refs: widen(1.0 / total_pix, *refs), out_shape=(ja...  2.57 us

profile of v5, /device:TPU:1, one launch (start us, length us, event | category | flops | bytes accessed | tf_op | source)
XLA Modules:
  0.0 82.7 jit_solution(13320121506673054755)
XLA Ops:
  0.6 79.5 %aspp.1 = (f32[2,9,8,256]{3,2,1,0:T(8,128)}, bf16[2,4,4,4,16,256]{5,4,3,2,1,0:T(8,128)(2,1)}, f32[16,256]{1,0:T(8,128)}) custom-call(bf16[672,1024]{1,0:T(8,128)(2,1)} %bitcast.8, s32[12,1,56]{2,1,0:T(1,128)} %bitcast.11, bf16[1024,256]{1,0:T(8,128)(2,1)} %refs_2_.1, bf16[2,3,3,1024,256]{4,3,2,1,0:T(8,128)(2,1)} %refs_3_.1, bf16[3,256,256]{2,1,0:T(8,128)(2,1)} %bitcast.10, ...), custom_call_target="tpu_custom_call" | custom-call | tf_op jit(solution)/shard_map/aspp/pallas_call | solution.py:567
  80.1 2.6 %widen.1 = (f32[2,9,8,256]{3,2,1,0:T(8,128)}, f32[1024,256]{1,0:T(8,128)}, f32[768,256]{1,0:T(8,128)}, f32[3,256]{1,0:T(4,128)}, f32[1,1]{1,0:T(1,128)}) custom-call(f32[2,9,8,256]{3,2,1,0:T(8,128)} %get-tuple-element.13.refs_0_, bf16[2,1024,256]{2,1,0:T(8,128)(2,1)} %bitcast.9, f32[16,256]{1,0:T(8,128)} %get-tuple-element.15.refs_2_), custom_call_target="tpu_custom_call" | custom-call | tf_op jit(solution)/shard_map/widen/pallas_call | solution.py:594

commit v6 on v5

--- a/solution.py
+++ b/solution.py
@@ -71,7 +71,7 @@
     rate = 12 + 6 * core
     k = 2 + core
 
-    counter = [UNITS * 12 + 13]
+    counter = [UNITS * 12 + 17]
 
     def remote(src, dst, to, i=None, sent=None):
         if i is None:
@@ -173,14 +173,24 @@
         middle(theirs + q)
         outer(theirs + q)
 
-    def halo(j):
+    def halo(j, h):
+        rows = block(XB + jnp.where(s == 0, 2, 0) + j)
         to = block(jnp.where(s == 0, j, XB + 4 + j))
-        return remote(feat.at[j * BLK : (j + 1) * BLK], xbuf.at[to], (dp, (1 - s) * 2 + j), UNITS * 12 + 4 + j)
-
-    @pl.when(core == 1 - s)
-    def _():
-        for j in range(2):
-            halo(j).start()
+        lanes = slice(h * 512, h * 512 + 512)
+        i = UNITS * 12 + 4 + h
+        return remote(xbuf.at[rows, lanes], xbuf.at[to, lanes], (dp, (1 - s) * 2 + j), i, UNITS * 12 + 13 + 2 * j + h)
+
+    def haloes(body):
+        @pl.when(core == s)
+        def _():
+            for j, h in ((0, 0), (0, 1), (1, 0)):
+                body(halo(j, h))
+
+        @pl.when(core == 1 - s)
+        def _():
+            body(halo(1, 1))
+
+    haloes(lambda copy: copy.start())
 
     @pl.loop(0, 4)
     def _(i):
@@ -288,7 +298,16 @@
         ext[1, to, :] = rounded.astype(BF)
         ext[2, to, :] = from_left(rounded).astype(BF)
 
+    def first_grad(first):
+        @pl.when(core == 1)
+        def _():
+            @pl.loop(0, 2)
+            def _(q):
+                rows = block(first + q)
+                db0[rows, :] = (mm_t(dh[rows, :], w_proj[0]) * slope(pre0[rows, :])).astype(BF)
+
     pl.loop(0, 2)(lambda q: branch_grad(mine + q))
+    first_grad(mine)
     dh_copy.wait_recv()
     pl.loop(0, 2)(lambda q: branch_grad(theirs + q))
 
@@ -363,7 +382,6 @@
             fin[u] = value
 
     mids = [plan(b, ORDER[b], True) for b in range(3)]
-    outers = [plan(3 + 3 * g + b, ORDER[b], True) for b in range(3) for g in range(2)]
     nears = [plan(3 + 3 * s + b, ORDER[b], True) for b in range(3)]
     fars = [plan(3 + 3 * (1 - s) + b, ORDER[b], True) for b in range(3)]
     smalls = plan(9, SMALL, False)
@@ -380,16 +398,13 @@
 
     everyone = pl.ds(XB * BLK, CHIP)
 
+    first_grad(theirs)
+
     @pl.when(core == 1)
     def _():
         for n in range(2):
             pbuf[n] = proj_grad(2 * n)
             p_copies[n].start()
-
-        @pl.loop(0, 4)
-        def _(i):
-            value = mm_t(dh[block(i), :], w_proj[0]) * slope(pre0[block(i), :])
-            db0[block(i), :] = value.astype(BF)
 
         tap(9, everyone, db0[...])
 
@@ -408,6 +423,12 @@
     for b in range(3):
         tap(b, everyone, ext[b, rows_from(BASE, 4), :])
         send(mids[b], 0)
+    passed_rows = block(jnp.where(s == 0, XB + 4, 0) + core)
+    for h in range(2):
+        lanes = slice(h * 512, h * 512 + 512)
+        remote(xbuf.at[passed_rows, lanes], xbuf.at[passed_rows, lanes], across, UNITS * 12 + 4 + h).wait_recv()
+    passed = go(remote(xbuf.at[passed_rows], xbuf.at[passed_rows], partner, UNITS * 12 + 6))
+
     small_step(0)
 
     @pl.when(core == 1)
@@ -419,19 +440,12 @@
         ext[1, to, :] = hraw[...]
         ext[2, to, :] = from_left(value).astype(BF)
 
-    passed_rows = block(jnp.where(s == 0, XB + 4, 0) + core)
-    remote(feat.at[0:BLK], xbuf.at[passed_rows], across, UNITS * 12 + 4 + core).wait_recv()
-    passed = go(remote(xbuf.at[passed_rows], xbuf.at[passed_rows], partner, UNITS * 12 + 6))
-
     for b in range(3):
         x_at = XB + jnp.where(s == 0, 0, 2)
         g_at = BASE + jnp.where(s == 0, k, 2 - k)
         tap(nears[b][0], rows_from(x_at, 2), ext[b, rows_from(g_at, 2), :])
         send(nears[b], 0)
 
-    for unit in mids:
-        forward(unit)
-    settle(smalls, 0)
     passed.wait_recv()
     for b in range(3):
         for n in range(2):
@@ -442,9 +456,19 @@
                 tap(fars[b][0], rows_from(x_at, 4 - n), ext[b, rows_from(g_at, 4 - n), :])
         send(fars[b], 0)
 
+    for unit in mids:
+        forward(unit)
+    settle(smalls, 0)
+    for unit in nears:
+        forward(unit)
+    for unit in mids:
+        settle(unit, 0)
     settle(smalls, 1)
-    for unit in outers:
+    for unit in fars:
         forward(unit)
+    small_step(1)
+    for unit in nears:
+        settle(unit, 0)
     settle(smalls, 2)
 
     eout[core, cx, cz, cy] = fin[9].astype(BF)
@@ -464,29 +488,30 @@
 
     gather_next(0)
     for unit in mids:
+        settle(unit, 1)
+    for unit in fars:
         settle(unit, 0)
-    small_step(1)
     gather_next(1)
-    for unit in outers:
-        settle(unit, 0)
-    gather_next(2)
-    for unit in mids:
-        settle(unit, 1)
     small_step(2)
-    for unit in outers:
-        settle(unit, 1)
-    gather_next(3)
-    e_swap = go(remote(eout.at[core], eout.at[core], partner))
     for unit in mids:
         settle(unit, 2)
-    for unit in outers:
+    for unit in nears:
+        settle(unit, 1)
+    for unit in fars:
+        settle(unit, 1)
+    gather_next(2)
+    small_step(3)
+    for unit in nears:
+        settle(unit, 2)
+    for unit in fars:
         settle(unit, 2)
 
     give = pl.ds(pl.multiple_of((1 - core) * 8, 8), 8)
     keep = pl.ds(pl.multiple_of(core * 8, 8), 8)
     swap[0] = fin[0:9, give, :]
     f_swap = go(remote(swap.at[0], swap.at[1], partner))
-    small_step(3)
+    gather_next(3)
+    e_swap = go(remote(eout.at[core], eout.at[core], partner))
 
     e_swap.wait_recv()
     f_swap.wait_recv()
@@ -497,10 +522,7 @@
 
     crossing(lambda g, t, m: cross_copy(t, g).wait_send())
 
-    @pl.when(core == 1 - s)
-    def _():
-        for j in range(2):
-            halo(j).wait_send()
+    haloes(lambda copy: copy.wait_send())
 
     @pl.when(core == 1)
     def _():

time: 82.9 us -> 83 us (level)
  no operation moved by 1% of the time
where the time goes in v6:
time: 83 us; the launch traced here: 82.8 us
  Pallas kernels  82.2 us (99%)
    pallas_call x1, Pallas kernels, on_device(): pl.pallas_call(lambda *refs: kernel(1.0 / math.sqrt(total_pix), *refs), o...  79.6 us
    pallas_call x1, Pallas kernels, on_device(): pl.pallas_call(lambda *refs: widen(1.0 / total_pix, *refs), out_shape=(ja...  2.57 us

profile of v6, /device:TPU:1, one launch (start us, length us, event | category | flops | bytes accessed | tf_op | source)
XLA Modules:
  0.0 82.8 jit_solution(7140890225831279852)
XLA Ops:
  0.6 79.6 %aspp.1 = (f32[2,9,8,256]{3,2,1,0:T(8,128)}, bf16[2,4,4,4,16,256]{5,4,3,2,1,0:T(8,128)(2,1)}, f32[16,256]{1,0:T(8,128)}) custom-call(bf16[672,1024]{1,0:T(8,128)(2,1)} %bitcast.8, s32[12,1,56]{2,1,0:T(1,128)} %bitcast.11, bf16[1024,256]{1,0:T(8,128)(2,1)} %refs_2_.1, bf16[2,3,3,1024,256]{4,3,2,1,0:T(8,128)(2,1)} %refs_3_.1, bf16[3,256,256]{2,1,0:T(8,128)(2,1)} %bitcast.10, ...), custom_call_target="tpu_custom_call" | custom-call | tf_op jit(solution)/shard_map/aspp/pallas_call | solution.py:589
  80.2 2.6 %widen.1 = (f32[2,9,8,256]{3,2,1,0:T(8,128)}, f32[1024,256]{1,0:T(8,128)}, f32[768,256]{1,0:T(8,128)}, f32[3,256]{1,0:T(4,128)}, f32[1,1]{1,0:T(1,128)}) custom-call(f32[2,9,8,256]{3,2,1,0:T(8,128)} %get-tuple-element.13.refs_0_, bf16[2,1024,256]{2,1,0:T(8,128)(2,1)} %bitcast.9, f32[16,256]{1,0:T(8,128)} %get-tuple-element.15.refs_2_), custom_call_target="tpu_custom_call" | custom-call | tf_op jit(solution)/shard_map/widen/pallas_call | solution.py:616

commit v7 on v6

--- a/solution.py
+++ b/solution.py
@@ -16,8 +16,9 @@
 CHIP = 24 * WIDTH
 BASE = 1
 XB = 2
-ORDER = ("xzy", "zyx", "yxz")
-SMALL = "yzx"
+MIDDLE = ("xzy", "zyx", "zxy")
+OUTER = ("xzy", "zyx", "yxz")
+SMALL = "xyz"
 AXES = "xzy"
 
 
@@ -381,10 +382,10 @@
         else:
             fin[u] = value
 
-    mids = [plan(b, ORDER[b], True) for b in range(3)]
-    nears = [plan(3 + 3 * s + b, ORDER[b], True) for b in range(3)]
-    fars = [plan(3 + 3 * (1 - s) + b, ORDER[b], True) for b in range(3)]
-    smalls = plan(9, SMALL, False)
+    mids = [plan(b, MIDDLE[b], True) for b in range(3)]
+    nears = [plan(3 + 3 * s + b, OUTER[b], True) for b in range(3)]
+    fars = [plan(3 + 3 * (1 - s) + b, OUTER[b], True) for b in range(3)]
+    smalls = plan(9, SMALL, True)
 
     def proj_grad(b):
         return t_mm(joined[b], dh[...]).astype(BF).reshape(4, 4, 16, 256)
@@ -398,6 +399,14 @@
 
     everyone = pl.ds(XB * BLK, CHIP)
 
+    def rows_from(m, count):
+        return pl.ds(pl.multiple_of(m * BLK, 16), count * BLK)
+
+    def middle_tap(b):
+        tap(b, everyone, ext[b, rows_from(BASE, 4), :])
+        send(mids[b], 0)
+
+    middle_tap(0)
     first_grad(theirs)
 
     @pl.when(core == 1)
@@ -416,13 +425,8 @@
             p_copies[n].wait_recv()
 
     send(smalls, 0)
-
-    def rows_from(m, count):
-        return pl.ds(pl.multiple_of(m * BLK, 16), count * BLK)
-
-    for b in range(3):
-        tap(b, everyone, ext[b, rows_from(BASE, 4), :])
-        send(mids[b], 0)
+    middle_tap(1)
+    middle_tap(2)
     passed_rows = block(jnp.where(s == 0, XB + 4, 0) + core)
     for h in range(2):
         lanes = slice(h * 512, h * 512 + 512)
@@ -455,6 +459,8 @@
                 g_at = BASE + jnp.where(s == 0, 0, n)
                 tap(fars[b][0], rows_from(x_at, 4 - n), ext[b, rows_from(g_at, 4 - n), :])
         send(fars[b], 0)
+        if b == 0:
+            forward(smalls)
 
     for unit in mids:
         forward(unit)
@@ -467,8 +473,6 @@
     for unit in fars:
         forward(unit)
     small_step(1)
-    for unit in nears:
-        settle(unit, 0)
     settle(smalls, 2)
 
     eout[core, cx, cz, cy] = fin[9].astype(BF)
@@ -487,20 +491,24 @@
             go(copy)
 
     gather_next(0)
+    for unit in nears:
+        settle(unit, 0)
     for unit in mids:
         settle(unit, 1)
+    gather_next(1)
     for unit in fars:
         settle(unit, 0)
-    gather_next(1)
     small_step(2)
+    for unit in nears:
+        settle(unit, 1)
+    gather_next(2)
     for unit in mids:
         settle(unit, 2)
-    for unit in nears:
-        settle(unit, 1)
     for unit in fars:
         settle(unit, 1)
-    gather_next(2)
     small_step(3)
+    gather_next(3)
+    e_swap = go(remote(eout.at[core], eout.at[core], partner))
     for unit in nears:
         settle(unit, 2)
     for unit in fars:
@@ -510,8 +518,6 @@
     keep = pl.ds(pl.multiple_of(core * 8, 8), 8)
     swap[0] = fin[0:9, give, :]
     f_swap = go(remote(swap.at[0], swap.at[1], partner))
-    gather_next(3)
-    e_swap = go(remote(eout.at[core], eout.at[core], partner))
 
     e_swap.wait_recv()
     f_swap.wait_recv()

time: 83 us -> 81.9 us (0.987)
  Pallas kernels: 82.2 us -> 81.2 us
    pallas_call x1, Pallas kernels: 79.6 us -> 78.6 us  [on_device(): pl.pallas_call(lambda *refs: kernel(1.0 / math.sqrt(total_pix), *refs), o...]
where the time goes in v7:
time: 81.9 us; the launch traced here: 81.8 us
  Pallas kernels  81.2 us (99%)
    pallas_call x1, Pallas kernels, on_device(): pl.pallas_call(lambda *refs: kernel(1.0 / math.sqrt(total_pix), *refs), o...  78.6 us
    pallas_call x1, Pallas kernels, on_device(): pl.pallas_call(lambda *refs: widen(1.0 / total_pix, *refs), out_shape=(ja...  2.57 us

profile of v7, /device:TPU:1, one launch (start us, length us, event | category | flops | bytes accessed | tf_op | source)
XLA Modules:
  0.0 81.8 jit_solution(10000696058625168931)
XLA Ops:
  0.6 78.6 %aspp.1 = (f32[2,9,8,256]{3,2,1,0:T(8,128)}, bf16[2,4,4,4,16,256]{5,4,3,2,1,0:T(8,128)(2,1)}, f32[16,256]{1,0:T(8,128)}) custom-call(bf16[672,1024]{1,0:T(8,128)(2,1)} %bitcast.8, s32[12,1,56]{2,1,0:T(1,128)} %bitcast.11, bf16[1024,256]{1,0:T(8,128)(2,1)} %refs_2_.1, bf16[2,3,3,1024,256]{4,3,2,1,0:T(8,128)(2,1)} %refs_3_.1, bf16[3,256,256]{2,1,0:T(8,128)(2,1)} %bitcast.10, ...), custom_call_target="tpu_custom_call" | custom-call | tf_op jit(solution)/shard_map/aspp/pallas_call | solution.py:595
  79.2 2.6 %widen.1 = (f32[2,9,8,256]{3,2,1,0:T(8,128)}, f32[1024,256]{1,0:T(8,128)}, f32[768,256]{1,0:T(8,128)}, f32[3,256]{1,0:T(4,128)}, f32[1,1]{1,0:T(1,128)}) custom-call(f32[2,9,8,256]{3,2,1,0:T(8,128)} %get-tuple-element.13.refs_0_, bf16[2,1024,256]{2,1,0:T(8,128)(2,1)} %bitcast.9, f32[16,256]{1,0:T(8,128)} %get-tuple-element.15.refs_2_), custom_call_target="tpu_custom_call" | custom-call | tf_op jit(solution)/shard_map/widen/pallas_call | solution.py:622

commit v8 on v7

--- a/solution.py
+++ b/solution.py
@@ -48,7 +48,7 @@
     feat, labels, w_one_h, w_atr_h, w_proj, w_cls,
     o_atr, eout, o_cls,
     xbuf, wbuf, wtow, wone, tacc, pre, pre0, cs, cr, joined, dh, ext, db0, raw, hraw,
-    s1, r1, s2, r2, s3, r3, fin, pbuf, clbuf, swap, lab,
+    s1, r1, s2, r2, s3, r3, rp, fin, pbuf, clbuf, swap, lab,
     lsem, ssem, rsem,
 ):
     dp = lax.axis_index("dp")
@@ -103,7 +103,12 @@
     one_local.start()
 
     barrier = pltpu.get_barrier_semaphore()
-    greet = [partner, beyond] + [peer(axis, d) for axis in AXES for d in (1, 2, 3)]
+    around = [(dz, dy) for dz in (2, 1, 3, 0) for dy in (2, 1, 3, 0) if dz or dy]
+
+    def aside(dz, dy):
+        return place(cx, (cz + dz) % 4, (cy + dy) % 4, core)
+
+    greet = [partner, beyond] + [peer("x", d) for d in (1, 2, 3)] + [aside(*at) for at in around]
     for other in greet:
         pl.semaphore_signal(barrier, inc=1, device_id=other, device_id_type=MESH)
 
@@ -378,7 +383,11 @@
         if phase < 2:
             into = (s2, s3)[phase]
             into[u] = value.astype(into.dtype)
-            send(unit, phase + 1)
+            if unit is smalls:
+                for copy in plane:
+                    go(copy)
+            else:
+                send(unit, phase + 1)
         else:
             fin[u] = value
 
@@ -386,6 +395,9 @@
     nears = [plan(3 + 3 * s + b, OUTER[b], True) for b in range(3)]
     fars = [plan(3 + 3 * (1 - s) + b, OUTER[b], True) for b in range(3)]
     smalls = plan(9, SMALL, True)
+    plane = [
+        remote(s2.at[9, (cz + dz) % 4, (cy + dy) % 4], rp.at[dz * 4 + dy - 1], aside(dz, dy)) for dz, dy in around
+    ]
 
     def proj_grad(b):
         return t_mm(joined[b], dh[...]).astype(BF).reshape(4, 4, 16, 256)
@@ -428,10 +440,11 @@
     middle_tap(1)
     middle_tap(2)
     passed_rows = block(jnp.where(s == 0, XB + 4, 0) + core)
+    passed = []
     for h in range(2):
-        lanes = slice(h * 512, h * 512 + 512)
-        remote(xbuf.at[passed_rows, lanes], xbuf.at[passed_rows, lanes], across, UNITS * 12 + 4 + h).wait_recv()
-    passed = go(remote(xbuf.at[passed_rows], xbuf.at[passed_rows], partner, UNITS * 12 + 6))
+        piece = xbuf.at[passed_rows, slice(h * 512, h * 512 + 512)]
+        remote(piece, piece, across, UNITS * 12 + 4 + h).wait_recv()
+        passed.append(go(remote(piece, piece, partner)))
 
     small_step(0)
 
@@ -450,7 +463,8 @@
         tap(nears[b][0], rows_from(x_at, 2), ext[b, rows_from(g_at, 2), :])
         send(nears[b], 0)
 
-    passed.wait_recv()
+    for copy in passed:
+        copy.wait_recv()
     for b in range(3):
         for n in range(2):
             @pl.when(core == n)
@@ -469,45 +483,41 @@
         forward(unit)
     for unit in mids:
         settle(unit, 0)
-    settle(smalls, 1)
     for unit in fars:
         forward(unit)
     small_step(1)
-    settle(smalls, 2)
-
-    eout[core, cx, cz, cy] = fin[9].astype(BF)
-    everything = slice(None)
-
-    def gather(axis, at):
-        view = eout.at[(core,) + at]
-        return [remote(view, view, peer(axis, d)) for d in (2, 1, 3)]
-
-    gathers = [gather("z", (cx, cz, cy)), gather("y", (cx, everything, cy)), gather("x", (cx, everything, everything))]
-
-    def gather_next(n):
-        for copy in gathers[n - 1] if n else ():
-            copy.wait_recv()
-        for copy in gathers[n] if n < 3 else ():
-            go(copy)
-
-    gather_next(0)
+
+    for copy in plane:
+        copy.wait_recv()
+    value = s2[9, cz, cy].astype(F32)
+    for n in range(15):
+        value = value + rp[n].astype(F32)
+    eout[core, cx, cz, cy] = value.astype(BF)
+    share, slab = eout.at[core, cx, cz, cy], eout.at[core, cx]
+    gather_plane = [remote(share, share, aside(dz, dy)) for dz, dy in around]
+    gather_x = [remote(slab, slab, peer("x", d)) for d in (2, 1, 3)]
+    for copy in gather_plane:
+        go(copy)
     for unit in nears:
         settle(unit, 0)
     for unit in mids:
         settle(unit, 1)
-    gather_next(1)
+    for copy in gather_plane:
+        copy.wait_recv()
+    for copy in gather_x:
+        go(copy)
     for unit in fars:
         settle(unit, 0)
     small_step(2)
     for unit in nears:
         settle(unit, 1)
-    gather_next(2)
     for unit in mids:
         settle(unit, 2)
     for unit in fars:
         settle(unit, 1)
     small_step(3)
-    gather_next(3)
+    for copy in gather_x:
+        copy.wait_recv()
     e_swap = go(remote(eout.at[core], eout.at[core], partner))
     for unit in nears:
         settle(unit, 2)
@@ -548,7 +558,7 @@
     assert counter[0] <= COPIES
 
 
-COPIES = 180
+COPIES = 210
 UNITS = 10
 
 
@@ -586,6 +596,7 @@
         ((UNITS, 3, 4, 16, 256), BF),
         ((UNITS, 4, 16, 256), F32),
         ((UNITS, 3, 16, 256), F32),
+        ((15, 16, 256), BF),
         ((UNITS, 16, 256), F32),
         ((2, 4, 4, 16, 256), BF),
         ((4, 4, 16, 256), F32),

time: 81.9 us -> 84.3 us (1.029)
  Pallas kernels: 81.2 us -> 83.5 us
    pallas_call x1, Pallas kernels: 78.6 us -> 80.9 us  [on_device(): pl.pallas_call(lambda *refs: kernel(1.0 / math.sqrt(total_pix), *refs), o...]
where the time goes in v8:
time: 84.3 us; the launch traced here: 84.2 us
  Pallas kernels  83.5 us (99%)
    pallas_call x1, Pallas kernels, on_device(): pl.pallas_call(lambda *refs: kernel(1.0 / math.sqrt(total_pix), *refs), o...  80.9 us
    pallas_call x1, Pallas kernels, on_device(): pl.pallas_call(lambda *refs: widen(1.0 / total_pix, *refs), out_shape=(ja...  2.57 us

profile of v8, /device:TPU:1, one launch (start us, length us, event | category | flops | bytes accessed | tf_op | source)
XLA Modules:
  0.0 84.2 jit_solution(14156606562961405062)
XLA Ops:
  0.6 80.9 %aspp.1 = (f32[2,9,8,256]{3,2,1,0:T(8,128)}, bf16[2,4,4,4,16,256]{5,4,3,2,1,0:T(8,128)(2,1)}, f32[16,256]{1,0:T(8,128)}) custom-call(bf16[672,1024]{1,0:T(8,128)(2,1)} %bitcast.8, s32[12,1,56]{2,1,0:T(1,128)} %bitcast.11, bf16[1024,256]{1,0:T(8,128)(2,1)} %refs_2_.1, bf16[2,3,3,1024,256]{4,3,2,1,0:T(8,128)(2,1)} %refs_3_.1, bf16[3,256,256]{2,1,0:T(8,128)(2,1)} %bitcast.10, ...), custom_call_target="tpu_custom_call" | custom-call | tf_op jit(solution)/shard_map/aspp/pallas_call | solution.py:606
  81.6 2.6 %widen.1 = (f32[2,9,8,256]{3,2,1,0:T(8,128)}, f32[1024,256]{1,0:T(8,128)}, f32[768,256]{1,0:T(8,128)}, f32[3,256]{1,0:T(4,128)}, f32[1,1]{1,0:T(1,128)}) custom-call(f32[2,9,8,256]{3,2,1,0:T(8,128)} %get-tuple-element.13.refs_0_, bf16[2,1024,256]{2,1,0:T(8,128)(2,1)} %bitcast.9, f32[16,256]{1,0:T(8,128)} %get-tuple-element.15.refs_2_), custom_call_target="tpu_custom_call" | custom-call | tf_op jit(solution)/shard_map/widen/pallas_call | solution.py:633

commit v9 on v7

--- a/solution.py
+++ b/solution.py
@@ -385,7 +385,7 @@
     mids = [plan(b, MIDDLE[b], True) for b in range(3)]
     nears = [plan(3 + 3 * s + b, OUTER[b], True) for b in range(3)]
     fars = [plan(3 + 3 * (1 - s) + b, OUTER[b], True) for b in range(3)]
-    smalls = plan(9, SMALL, True)
+    smalls = plan(9, SMALL, False)
 
     def proj_grad(b):
         return t_mm(joined[b], dh[...]).astype(BF).reshape(4, 4, 16, 256)
@@ -406,7 +406,6 @@
         tap(b, everyone, ext[b, rows_from(BASE, 4), :])
         send(mids[b], 0)
 
-    middle_tap(0)
     first_grad(theirs)
 
     @pl.when(core == 1)
@@ -425,6 +424,7 @@
             p_copies[n].wait_recv()
 
     send(smalls, 0)
+    middle_tap(0)
     middle_tap(1)
     middle_tap(2)
     passed_rows = block(jnp.where(s == 0, XB + 4, 0) + core)
@@ -459,20 +459,17 @@
                 g_at = BASE + jnp.where(s == 0, 0, n)
                 tap(fars[b][0], rows_from(x_at, 4 - n), ext[b, rows_from(g_at, 4 - n), :])
         send(fars[b], 0)
-        if b == 0:
-            forward(smalls)
-
+
+    settle(smalls, 0)
     for unit in mids:
         forward(unit)
-    settle(smalls, 0)
     for unit in nears:
         forward(unit)
+    settle(smalls, 1)
     for unit in mids:
         settle(unit, 0)
-    settle(smalls, 1)
     for unit in fars:
         forward(unit)
-    small_step(1)
     settle(smalls, 2)
 
     eout[core, cx, cz, cy] = fin[9].astype(BF)
@@ -491,26 +488,27 @@
             go(copy)
 
     gather_next(0)
+    small_step(1)
     for unit in nears:
         settle(unit, 0)
+    gather_next(1)
     for unit in mids:
         settle(unit, 1)
-    gather_next(1)
     for unit in fars:
         settle(unit, 0)
+    gather_next(2)
     small_step(2)
     for unit in nears:
         settle(unit, 1)
-    gather_next(2)
     for unit in mids:
         settle(unit, 2)
     for unit in fars:
         settle(unit, 1)
     small_step(3)
+    for unit in nears:
+        settle(unit, 2)
     gather_next(3)
     e_swap = go(remote(eout.at[core], eout.at[core], partner))
-    for unit in nears:
-        settle(unit, 2)
     for unit in fars:
         settle(unit, 2)
 

time: 81.9 us -> 80.8 us (0.987)
  Pallas kernels: 81.2 us -> 80 us
    pallas_call x1, Pallas kernels: 78.6 us -> 77.4 us  [on_device(): pl.pallas_call(lambda *refs: kernel(1.0 / math.sqrt(total_pix), *refs), o...]
where the time goes in v9:
time: 80.8 us; the launch traced here: 80.7 us
  Pallas kernels  80 us (99%)
    pallas_call x1, Pallas kernels, on_device(): pl.pallas_call(lambda *refs: kernel(1.0 / math.sqrt(total_pix), *refs), o...  77.4 us
    pallas_call x1, Pallas kernels, on_device(): pl.pallas_call(lambda *refs: widen(1.0 / total_pix, *refs), out_shape=(ja...  2.57 us

profile of v9, /device:TPU:1, one launch (start us, length us, event | category | flops | bytes accessed | tf_op | source)
XLA Modules:
  0.0 80.7 jit_solution(8650089045593762717)
XLA Ops:
  0.6 77.4 %aspp.1 = (f32[2,9,8,256]{3,2,1,0:T(8,128)}, bf16[2,4,4,4,16,256]{5,4,3,2,1,0:T(8,128)(2,1)}, f32[16,256]{1,0:T(8,128)}) custom-call(bf16[672,1024]{1,0:T(8,128)(2,1)} %bitcast.8, s32[12,1,56]{2,1,0:T(1,128)} %bitcast.11, bf16[1024,256]{1,0:T(8,128)(2,1)} %refs_2_.1, bf16[2,3,3,1024,256]{4,3,2,1,0:T(8,128)(2,1)} %refs_3_.1, bf16[3,256,256]{2,1,0:T(8,128)(2,1)} %bitcast.10, ...), custom_call_target="tpu_custom_call" | custom-call | tf_op jit(solution)/shard_map/aspp/pallas_call | solution.py:593
  78.1 2.6 %widen.1 = (f32[2,9,8,256]{3,2,1,0:T(8,128)}, f32[1024,256]{1,0:T(8,128)}, f32[768,256]{1,0:T(8,128)}, f32[3,256]{1,0:T(4,128)}, f32[1,1]{1,0:T(1,128)}) custom-call(f32[2,9,8,256]{3,2,1,0:T(8,128)} %get-tuple-element.13.refs_0_, bf16[2,1024,256]{2,1,0:T(8,128)(2,1)} %bitcast.9, f32[16,256]{1,0:T(8,128)} %get-tuple-element.15.refs_2_), custom_call_target="tpu_custom_call" | custom-call | tf_op jit(solution)/shard_map/widen/pallas_call | solution.py:620

commit v10 on v9

--- a/solution.py
+++ b/solution.py
@@ -406,14 +406,12 @@
         tap(b, everyone, ext[b, rows_from(BASE, 4), :])
         send(mids[b], 0)
 
-    first_grad(theirs)
-
     @pl.when(core == 1)
     def _():
         for n in range(2):
             pbuf[n] = proj_grad(2 * n)
             p_copies[n].start()
-
+        first_grad(theirs)
         tap(9, everyone, db0[...])
 
     @pl.when(core == 0)
@@ -428,10 +426,11 @@
     middle_tap(1)
     middle_tap(2)
     passed_rows = block(jnp.where(s == 0, XB + 4, 0) + core)
+    passed = []
     for h in range(2):
-        lanes = slice(h * 512, h * 512 + 512)
-        remote(xbuf.at[passed_rows, lanes], xbuf.at[passed_rows, lanes], across, UNITS * 12 + 4 + h).wait_recv()
-    passed = go(remote(xbuf.at[passed_rows], xbuf.at[passed_rows], partner, UNITS * 12 + 6))
+        piece = xbuf.at[passed_rows, slice(h * 512, h * 512 + 512)]
+        remote(piece, piece, across, UNITS * 12 + 4 + h).wait_recv()
+        passed.append(go(remote(piece, piece, partner)))
 
     small_step(0)
 
@@ -450,7 +449,8 @@
         tap(nears[b][0], rows_from(x_at, 2), ext[b, rows_from(g_at, 2), :])
         send(nears[b], 0)
 
-    passed.wait_recv()
+    for copy in passed:
+        copy.wait_recv()
     for b in range(3):
         for n in range(2):
             @pl.when(core == n)

time: 80.8 us -> 82 us (1.015)
  Pallas kernels: 80 us -> 81.2 us
    pallas_call x1, Pallas kernels: 77.4 us -> 78.6 us  [on_device(): pl.pallas_call(lambda *refs: kernel(1.0 / math.sqrt(total_pix), *refs), o...]
where the time goes in v10:
time: 82 us; the launch traced here: 81.8 us
  Pallas kernels  81.2 us (99%)
    pallas_call x1, Pallas kernels, on_device(): pl.pallas_call(lambda *refs: kernel(1.0 / math.sqrt(total_pix), *refs), o...  78.6 us
    pallas_call x1, Pallas kernels, on_device(): pl.pallas_call(lambda *refs: widen(1.0 / total_pix, *refs), out_shape=(ja...  2.57 us

profile of v10, /device:TPU:1, one launch (start us, length us, event | category | flops | bytes accessed | tf_op | source)
XLA Modules:
  0.0 81.8 jit_solution(5407492632612035452)
XLA Ops:
  0.6 78.6 %aspp.1 = (f32[2,9,8,256]{3,2,1,0:T(8,128)}, bf16[2,4,4,4,16,256]{5,4,3,2,1,0:T(8,128)(2,1)}, f32[16,256]{1,0:T(8,128)}) custom-call(bf16[672,1024]{1,0:T(8,128)(2,1)} %bitcast.8, s32[12,1,56]{2,1,0:T(1,128)} %bitcast.11, bf16[1024,256]{1,0:T(8,128)(2,1)} %refs_2_.1, bf16[2,3,3,1024,256]{4,3,2,1,0:T(8,128)(2,1)} %refs_3_.1, bf16[3,256,256]{2,1,0:T(8,128)(2,1)} %bitcast.10, ...), custom_call_target="tpu_custom_call" | custom-call | tf_op jit(solution)/shard_map/aspp/pallas_call | solution.py:593
  79.2 2.6 %widen.1 = (f32[2,9,8,256]{3,2,1,0:T(8,128)}, f32[1024,256]{1,0:T(8,128)}, f32[768,256]{1,0:T(8,128)}, f32[3,256]{1,0:T(4,128)}, f32[1,1]{1,0:T(1,128)}) custom-call(f32[2,9,8,256]{3,2,1,0:T(8,128)} %get-tuple-element.13.refs_0_, bf16[2,1024,256]{2,1,0:T(8,128)(2,1)} %bitcast.9, f32[16,256]{1,0:T(8,128)} %get-tuple-element.15.refs_2_), custom_call_target="tpu_custom_call" | custom-call | tf_op jit(solution)/shard_map/widen/pallas_call | solution.py:620
